TPU v7x, 256 devices: a whole 4x4x8 slice. The times are simulated.
256 devices in a mesh: pipe: 2 (over y_lo), dp: 16 (over z, y_hi), tensor: 8 (over x, core).
Axes of the slice: x: 4, y: 4 (y_hi: 2, y_lo: 2; y = y_hi * 2 + y_lo), z: 8, core: 2. Of those that a mesh axis runs over, the one named last changes fastest.
Arguments:
- handoff: bfloat16 [2, 32768, 1024], P('pipe', 'dp', 'tensor'), may hold values from -6 to 6
- hidden_pre: bfloat16 [2, 32768, 4096], P('pipe', 'dp', 'tensor'), may hold values from -6 to 6
- down_weight: bfloat16 [2, 4096, 1024], P('pipe', 'tensor'), may hold values from -6 to 6
- up_weight: bfloat16 [2, 4096, 1024], P('pipe', 'tensor'), may hold values from -6 to 6
- moment: float32 [2, 4096, 1024], P('pipe', ('tensor', 'dp')), may hold values from -3 to 3
- second: float32 [2, 4096, 1024], P('pipe', ('tensor', 'dp')), may hold values from 0.05 to 2
Outputs:
- input_grad: bfloat16 [2, 32768, 1024], P('pipe', 'dp', 'tensor')
- new_down: bfloat16 [2, 4096, 1024], P('pipe', 'tensor')
- new_moment: float32 [2, 4096, 1024], P('pipe', ('tensor', 'dp'))
- new_second: float32 [2, 4096, 1024], P('pipe', ('tensor', 'dp'))
All inputs are finite; a program needn't handle non-finite values.
Results may differ from a plain program's by a relative error of at most 0.017.
Values may be sent and summed in bfloat16 or wider, within the bound.
A program may use at most 64 MiB of HBM per device.

v0:
```python
import math

import jax
import jax.numpy as jnp
from jax import lax
from jax.sharding import PartitionSpec as P


def from_behind(block, axis, distance):
    devices = range(lax.axis_size(axis))
    route = [((i - distance) % len(devices), i) for i in devices]
    return lax.ppermute(block, axis, route)


def normal_cdf(inputs):
    return 0.5 * (1.0 + jax.scipy.special.erf(inputs * (1.0 / math.sqrt(2.0))))


def gelu_value(inputs):
    return inputs * normal_cdf(inputs)


def gelu_slope(inputs):
    return normal_cdf(inputs) + inputs * jnp.exp(-0.5 * inputs * inputs) * (
        1.0 / math.sqrt(2.0 * math.pi)
    )


def on_device(handoff, hidden_pre, down_weight, up_weight, moment, second):
    arrived = from_behind(handoff, "pipe", -1)
    incoming = lax.all_gather(arrived, "tensor", axis=2, tiled=True)
    incoming = incoming[0]
    tok_rows = incoming.shape[0]
    model_width = incoming.shape[1]
    slab_rows = down_weight.shape[1]
    shard_rows = moment.shape[1]
    hidden_total = slab_rows * lax.axis_size("tensor")
    token_total = tok_rows * lax.axis_size("dp")
    pre_values = hidden_pre[0].astype(jnp.float32)
    hidden = gelu_value(pre_values).astype(jnp.bfloat16)
    down_back = lax.dot_general(
        incoming, down_weight[0], (((1,), (1,)), ((), ())), preferred_element_type=jnp.float32
    )
    act_grad = (down_back * (1.0 / math.sqrt(model_width)) * gelu_slope(pre_values)).astype(
        jnp.bfloat16
    )
    partial_value = jnp.dot(act_grad, up_weight[0], preferred_element_type=jnp.float32) * (
        1.0 / math.sqrt(hidden_total)
    )
    summed = lax.psum(partial_value.astype(jnp.bfloat16), "tensor").astype(jnp.float32)
    col_width = model_width // lax.axis_size("tensor")
    own_cols = lax.dynamic_slice_in_dim(summed, lax.axis_index("tensor") * col_width, col_width, 1)
    input_grad = own_cols.astype(jnp.bfloat16)[None]
    grad_scale = 1.0 / math.sqrt(token_total)
    product = lax.dot_general(
        hidden, incoming, (((0,), (0,)), ((), ())), preferred_element_type=jnp.float32
    )
    gradient = lax.psum_scatter(
        (product * grad_scale).astype(jnp.bfloat16), "dp", scatter_dimension=0, tiled=True
    ).astype(jnp.float32)
    new_m = 0.9 * moment[0] + 0.1 * gradient
    new_v = 0.95 * second[0] + 0.05 * gradient * gradient
    own_rows = lax.dynamic_slice_in_dim(
        down_weight[0], lax.axis_index("dp") * shard_rows, shard_rows, 0
    )
    fresh_rows = (own_rows.astype(jnp.float32) - 0.2 * new_m / (jnp.sqrt(new_v) + 1e-08)).astype(
        jnp.bfloat16
    )
    new_down = lax.all_gather(fresh_rows, "dp", axis=0, tiled=True)
    return (input_grad, new_down[None], new_m[None], new_v[None])


def solution(mesh):
    placed = (
        P("pipe", "dp", "tensor"),
        P("pipe", "dp", "tensor"),
        P("pipe", "tensor", None),
        P("pipe", "tensor", None),
        P("pipe", ("tensor", "dp"), None),
        P("pipe", ("tensor", "dp"), None),
    )
    return jax.shard_map(
        on_device,
        mesh=mesh,
        in_specs=placed,
        out_specs=(
            P("pipe", "dp", "tensor"),
            P("pipe", "tensor", None),
            P("pipe", ("tensor", "dp"), None),
            P("pipe", ("tensor", "dp"), None),
        ),
        check_vma=False,
    )
```

profile of v0, /device:TPU:1, one launch (start us, length us, event | category | flops | bytes accessed | tf_op | source)
XLA Modules:
  0.0 439.9 jit_solution(3089107897146413912)
XLA Ops:
  7.2 0.0 copy-start
  7.2 0.0 all-gather.3.cloned.1.call-start
  7.2 2.2 collective-permute-start
  9.4 10.7 %collective-permute-done = bf16[1,2048,128]{2,1,0:T(8,128)(2,1)S(1)} collective-permute-done((bf16[1,2048,128]{2,1,0:T(8,128)(2,1)}, bf16[1,2048,128]{2,1,0:T(8,128)(2,1)S(1)}, u32[]{:S(2)}, u32[]{:S(2)}) %collective-permute-start) | collective-permute-done | bytes 524320 | tf_op jit(solution)/shard_map/ppermute | solution.py:12
  20.2 0.0 copy-start.1
  20.2 0.8 copy-done.1
  21.0 0.0 all-gather.3.cloned.1.call-update
  21.0 0.0 copy-start.4
  21.0 0.0 reduce-scatter.2.cloned.1.call-start
  21.0 43.9 %all-gather.3.cloned.1.call-done = bf16[1,2048,1024]{2,1,0:T(8,128)(2,1)} async-done(((bf16[1,2048,128]{2,1,0:T(8,128)(2,1)}), bf16[1,2048,1024]{2,1,0:T(8,128)(2,1)}) %all-gather.3.cloned.1.call-update) | async-done | bytes 4194320 | tf_op jit(solution)/shard_map/all_gather | solution.py:31
  65.0 6.2 %multiply_convert_fusion.1 = bf16[512,1024]{1,0:T(8,128)(2,1)} fusion(bf16[1,2048,1024]{2,1,0:T(8,128)(2,1)} %all-gather.3.cloned.1.call-done, bf16[1,2048,512]{2,1,0:T(8,128)(2,1)} %param.7), kind=kOutput, calls=%fused_computation.25 | convolution fusion | flops 2154823680 | bytes 7340032 | tf_op jit(solution)/shard_map/dot_general | solution.py:55
  71.1 0.0 reduce-scatter.2.cloned.1.call-update
  71.2 0.0 all-reduce.2.cloned.1.call-start
  71.2 0.0 copy-done
  71.2 0.0 copy-done.4
  71.2 9.2 %multiply_convert_fusion = bf16[2048,1024]{1,0:T(8,128)(2,1)} fusion(bf16[1,2048,512]{2,1,0:T(8,128)(2,1)} %param.7, bf16[1,2048,1024]{2,1,0:T(8,128)(2,1)} %all-gather.3.cloned.1.call-done, bf16[1,512,1024]{2,1,0:T(8,128)(2,1)S(1)} %copy-done, bf16[1,512,1024]{2,1,0:T(8,128)(2,1)S(1)} %copy-done.4), kind=kOutput, calls=%fused_computation | convolution fusion | flops 4311744512 | bytes 12582912 | tf_op jit(solution)/shard_map/dot_general | solution.py:47
  80.4 0.0 copy-start.2
  80.4 0.0 copy-start.3
  80.4 0.0 all-reduce.2.cloned.1.call-update
  80.4 0.0 all-gather.5.cloned.1.call-start
  80.5 189.4 %reduce-scatter.2.cloned.1.call-done = bf16[32,1024]{1,0:T(8,128)(2,1)} async-done(((bf16[512,1024]{1,0:T(8,128)(2,1)}), bf16[32,1024]{1,0:T(8,128)(2,1)}) %reduce-scatter.2.cloned.1.call-update) | async-done | bytes 65552 | tf_op jit(solution)/shard_map/reduce_scatter | solution.py:58
  269.9 0.0 copy-done.2
  269.9 0.0 copy-done.3
  269.9 1.6 fusion.41
  271.5 0.0 all-gather.5.cloned.1.call-update
  271.5 79.6 %all-reduce.2.cloned.1.call-done = bf16[2048,1024]{1,0:T(8,128)(2,1)} async-done(((bf16[2048,1024]{1,0:T(8,128)(2,1)}), bf16[2048,1024]{1,0:T(8,128)(2,1)}) %all-reduce.2.cloned.1.call-update) | async-done | bytes 4194320 | tf_op jit(solution)/shard_map/psum | solution.py:50
  351.1 1.9 fusion.36
  353.0 78.1 %all-gather.5.cloned.1.call-done = bf16[512,1024]{1,0:T(8,128)(2,1)} async-done(((bf16[32,1024]{1,0:T(8,128)(2,1)}), bf16[512,1024]{1,0:T(8,128)(2,1)}) %all-gather.5.cloned.1.call-update) | async-done | bytes 1048592 | tf_op jit(solution)/shard_map/all_gather | solution.py:69
  431.1 2.3 copy.12
Async XLA Ops:
  7.2 64.1 %copy-start = (bf16[1,512,1024]{2,1,0:T(8,128)(2,1)S(1)}, bf16[1,512,1024]{2,1,0:T(8,128)(2,1)}, u32[]{:S(2)}) copy-start(bf16[1,512,1024]{2,1,0:T(8,128)(2,1)} %param.9) | copy-start | bytes 3145732
  7.2 57.8 %all-gather.3.cloned.1.call-start = ((), (), s32[]{:S(2)}) async-start(), calls=%async_computation.1 | async-start | bytes 4718592 | tf_op jit(solution)/shard_map/all_gather | solution.py:31
  7.2 12.9 %collective-permute-start = (bf16[1,2048,128]{2,1,0:T(8,128)(2,1)}, bf16[1,2048,128]{2,1,0:T(8,128)(2,1)S(1)}, u32[]{:S(2)}, u32[]{:S(2)}) collective-permute-start(bf16[1,2048,128]{2,1,0:T(8,128)(2,1)} %param.6), channel_id=1, source_target_pairs={{128,0},{0,128},{129,1},{1,129},{130,2},{2,130},{131,3},{3,131},{1... | collective-permute-start | bytes 1572872 | tf_op jit(solution)/shard_map/ppermute | solution.py:12
  20.2 0.8 copy-start.1
  21.0 50.3 %copy-start.4 = (bf16[1,512,1024]{2,1,0:T(8,128)(2,1)S(1)}, bf16[1,512,1024]{2,1,0:T(8,128)(2,1)}, u32[]{:S(2)}) copy-start(bf16[1,512,1024]{2,1,0:T(8,128)(2,1)} %param.8) | copy-start | bytes 3145732
  21.0 248.9 %reduce-scatter.2.cloned.1.call-start = ((), (), s32[]{:S(2)}) async-start(), calls=%async_computation.3 | async-start | bytes 1114112 | tf_op jit(solution)/shard_map/reduce_scatter | solution.py:58
  71.2 280.0 %all-reduce.2.cloned.1.call-start = ((), (), s32[]{:S(2)}) async-start(), calls=%async_computation.2 | async-start | bytes 8388608 | tf_op jit(solution)/shard_map/psum | solution.py:50
  80.4 189.4 %copy-start.2 = (f32[1,32,1024]{2,1,0:T(8,128)S(1)}, f32[1,32,1024]{2,1,0:T(8,128)}, u32[]{:S(2)}) copy-start(f32[1,32,1024]{2,1,0:T(8,128)} %param.11) | copy-start | bytes 393220
  80.4 189.4 %copy-start.3 = (f32[1,32,1024]{2,1,0:T(8,128)S(1)}, f32[1,32,1024]{2,1,0:T(8,128)}, u32[]{:S(2)}) copy-start(f32[1,32,1024]{2,1,0:T(8,128)} %param.10) | copy-start | bytes 393220
  80.4 350.7 %all-gather.5.cloned.1.call-start = ((), (), s32[]{:S(2)}) async-start(), calls=%async_computation.4 | async-start | bytes 1114112 | tf_op jit(solution)/shard_map/all_gather | solution.py:69
Sparse Core Ops, SparseCore 0:
  21.1 43.8 all-gather.2
  71.3 198.5 reduce-scatter.1
  272.2 78.8 all-reduce.1
  354.2 76.9 all-gather.4
where the time goes:
time: 443 us; the launch traced here: 440 us
  waiting for transfers between devices  402 us (91%)
  matrix products  15.3 us (3%)
  between operations  13.8 us (3%)
    reduce_scatter x1, waiting for transfers between devices, on_device(): lax.psum_scatter((product * grad_scale).astype(jnp.bfloat16), 'dp', scatt...  189 us
    psum x1, waiting for transfers between devices, on_device(): lax.psum(partial_value.astype(jnp.bfloat16), 'tensor').astype(jnp.float32)  79.6 us
    all_gather x1, waiting for transfers between devices, on_device(): new_down = lax.all_gather(fresh_rows, 'dp', axis=0, tiled=True)  78.1 us
    all_gather x1, waiting for transfers between devices, on_device(): incoming = lax.all_gather(arrived, 'tensor', axis=2, tiled=True)  43.9 us
    ppermute x1, waiting for transfers between devices, from_behind(): return lax.ppermute(block, axis, route)  10.7 us
    dot_general x1, matrix products, on_device(): jnp.dot(act_grad, up_weight[0], preferred_element_type=jnp.float32)  9.17 us
  transfers between devices with their start and end apart: 5, of which 5 were waited for; matrix products, arithmetic and copies ran while one was open for 3% of the time, Pallas kernels for 0%

commit v1 on v0

v1 whole, which is shorter than its diff:
```python
import math

import jax
import jax.numpy as jnp
from jax import lax
from jax.experimental import pallas as pl
from jax.experimental.pallas import tpu as pltpu
from jax.sharding import PartitionSpec as P

F32 = jnp.float32
BF16 = jnp.bfloat16

X = 4
Z = 8
D = 1024
HW = 512
TOK = 2048
FF = 4096
TOKENS = 32768
ROWS = 32
PIECES = 4
PIECE = TOK // PIECES
CHUNKS = 8
CHUNK = TOK // CHUNKS
COLS = D // X
HALF = COLS // 2
N_SENDS = 200


def kernel(
    handoff, pre_in, down_in, up_in, moment_in, second_in,
    grad_out, down_out, moment_out, second_out,
    inc, pre, hidden_t, slope, down, up, moment, second,
    part, part_got, two_got, one_send, one_got, grad,
    term, up_got, dn_got, total, total_half, half_got, new_m, new_v, fresh,
    send, recv, local,
):
    p = lax.axis_index("pipe")
    d = lax.axis_index("dp")
    t = lax.axis_index("tensor")
    z, yh = lax.div(d, 2), lax.rem(d, 2)
    x, c = lax.div(t, 2), lax.rem(t, 2)

    def at_x(k):
        return lax.rem(x + (k + X), X)

    def at_z(k):
        return lax.rem(z + (k + Z), Z)

    across = (1 - p, d, t)
    core = (p, d, x * 2 + (1 - c))
    x_up = (p, d, at_x(1) * 2 + c)
    x_dn = (p, d, at_x(-1) * 2 + c)
    z_up = (p, at_z(1) * 2 + yh, t)
    z_dn = (p, at_z(-1) * 2 + yh, t)
    mate = (p, z * 2 + (1 - yh), t)
    partners = (across, core, x_up, x_dn, z_up, z_dn, mate)

    sent = []

    def put(src, dst, device):
        i = len(sent)
        copy = pltpu.make_async_remote_copy(
            src_ref=src, dst_ref=dst, send_sem=send.at[i], recv_sem=recv.at[i],
            device_id=device, device_id_type=pl.DeviceIdType.MESH,
        )
        copy.start()
        sent.append(copy)
        return copy

    stays = []

    def move(src, dst):
        copy = pltpu.make_async_copy(src, dst, local.at[len(stays)])
        copy.start()
        stays.append(copy)
        return copy

    barrier = pltpu.get_barrier_semaphore()
    for device in partners:
        pl.semaphore_signal(barrier, inc=1, device_id=device, device_id_type=pl.DeviceIdType.MESH)
    in_pre = move(pre_in.at[0], pre)
    in_down = move(down_in.at[0], down)
    in_up = move(up_in.at[0], up)
    in_moment = move(moment_in.at[0], moment)
    in_second = move(second_in.at[0], second)
    pl.semaphore_wait(barrier, len(partners))

    def piece(s):
        return pl.ds(s * PIECE, PIECE)

    slot_of = {k: at_x(k) * 2 + c for k in (0, -1, 1, 2)}
    y_got = [put(handoff.at[0, piece(s)], inc.at[t, piece(s)], across) for s in range(PIECES)]
    dn_piece, up_piece, two_piece, core_piece = {}, {}, {}, {}

    def share(k, s):
        block = inc.at[slot_of[k], piece(s)]
        core_piece[k, s] = put(block, block, core)

    def from_y(s):
        y_got[s].wait_recv()
        block = inc.at[slot_of[0], piece(s)]
        up_piece[s] = put(block, block, x_up)
        dn_piece[s] = put(block, block, x_dn)
        share(0, s)

    def from_below(s):
        up_piece[s].wait_recv()
        block = inc.at[slot_of[-1], piece(s)]
        if s % 2 == 0:
            two_piece[s] = put(block, block, x_up)
        share(-1, s)

    def from_above(s):
        dn_piece[s].wait_recv()
        block = inc.at[slot_of[1], piece(s)]
        if s % 2 == 1:
            two_piece[s] = put(block, block, x_dn)
        share(1, s)

    def from_two(s):
        two_piece[s].wait_recv()
        share(2, s)

    GELU = 128

    def gelu(first, last):
        def body(b, carry):
            rows = pl.ds(pl.multiple_of(b * GELU, GELU), GELU)
            a = pre[rows, :].astype(F32)
            cdf = 0.5 * (1.0 + lax.erf(a * (1.0 / math.sqrt(2.0))))
            slope[rows, :] = cdf + a * jnp.exp(-0.5 * a * a) * (1.0 / math.sqrt(2.0 * math.pi))
            hidden_t[:, rows] = (a * cdf).astype(BF16).T
            return carry

        lax.fori_loop(first, last, body, 0)

    up_sum, dn_sum, half_sum = {}, {}, {}

    def z_rows(k):
        return pl.ds(pl.multiple_of(at_z(k) * 2 * ROWS, 2 * ROWS), 2 * ROWS)

    def terms(k):
        for s in range(PIECES):
            core_piece[k, s].wait_recv()
        xa = at_x(k)
        block = jnp.concatenate([inc[xa * 2], inc[xa * 2 + 1]], axis=1)
        product = jnp.dot(hidden_t[...], block, preferred_element_type=F32)
        term[xa] = (product * (1.0 / math.sqrt(TOKENS))).astype(BF16)
        far = z_rows(4)
        lo, hi = pl.ds(0, HALF), pl.ds(HALF, HALF)
        up_sum[k] = put(term.at[xa, far, lo], up_got.at[xa, 0, :, lo], z_up)
        dn_sum[k] = put(term.at[xa, far, hi], dn_got.at[xa, 0, :, hi], z_dn)

    def add_rows(xa, rows, got, step, cols):
        mine = term[xa, rows, cols].astype(F32) + got[xa, step, :, cols].astype(F32)
        term[xa, rows, cols] = mine.astype(BF16)

    def z_step(k, j):
        xa = at_x(k)
        full = pl.ds(0, COLS)
        rows = z_rows(4 - j)
        up_sum[k].wait_recv()
        add_rows(xa, rows, up_got, j - 1, pl.ds(0, HALF) if j == 1 else full)
        up_sum[k] = put(term.at[xa, rows], up_got.at[xa, j], z_up)
        rows = z_rows(j - 4)
        dn_sum[k].wait_recv()
        add_rows(xa, rows, dn_got, j - 1, pl.ds(HALF, HALF) if j == 1 else full)
        dn_sum[k] = put(term.at[xa, rows], dn_got.at[xa, j], z_dn)

    def z_last(k):
        xa = at_x(k)
        up_sum[k].wait_recv()
        dn_sum[k].wait_recv()
        both = term[xa, z_rows(0)].astype(F32) + up_got[xa, 3].astype(F32) + dn_got[xa, 3].astype(F32)
        total[xa] = both
        total_half[xa] = both.astype(BF16)
        other = pl.ds(pl.multiple_of((1 - yh) * ROWS, ROWS), ROWS)
        half_sum[k] = put(total_half.at[xa, other], half_got.at[xa], mate)

    own_rows = pl.ds(pl.multiple_of(d * ROWS, ROWS), ROWS)

    def adam(k):
        xa = at_x(k)
        cols = pl.ds(pl.multiple_of(xa * COLS, COLS), COLS)
        half_sum[k].wait_recv()
        mine = pl.ds(pl.multiple_of(yh * ROWS, ROWS), ROWS)
        gradient = total[xa, mine] + half_got[xa].astype(F32)
        m = 0.9 * moment[:, cols] + 0.1 * gradient
        v = 0.95 * second[:, cols] + 0.05 * gradient * gradient
        new_m[:, cols] = m
        new_v[:, cols] = v
        old = down[own_rows, cols].astype(F32)
        fresh[own_rows, cols] = (old - 0.2 * m / (jnp.sqrt(v) + 1e-08)).astype(BF16)

    ring_up, ring_dn, side = {}, {}, {}

    def new_rows(k, h, first=0, count=ROWS):
        start = (at_z(k) * 2 + h) * ROWS + first
        return fresh.at[pl.ds(pl.multiple_of(start, count), count)]

    def spread(h, key):
        block = new_rows(0, h)
        ring_up[key] = put(block, block, z_up)
        ring_dn[key] = put(block, block, z_dn)

    def relay(h, key, j):
        part_rows = (0, ROWS) if j < 3 else (0, ROWS // 2)
        ring_up[key].wait_recv()
        block = new_rows(-j, h, *part_rows)
        ring_up[key] = put(block, block, z_up)
        part_rows = (0, ROWS) if j < 3 else (ROWS // 2, ROWS // 2)
        ring_dn[key].wait_recv()
        block = new_rows(j, h, *part_rows)
        ring_dn[key] = put(block, block, z_dn)

    pair, two, one_up, one_dn = {}, {}, {}, {}

    def chunk(i):
        return pl.ds(i * CHUNK, CHUNK)

    def partial(i):
        rows = chunk(i)
        block = jnp.concatenate([inc[s, rows] for s in range(2 * X)], axis=1)
        back = lax.dot_general(block, down[...], (((1,), (1,)), ((), ())), preferred_element_type=F32)
        act = (back * (1.0 / math.sqrt(D)) * slope[rows, :]).astype(BF16)
        value = jnp.dot(act, up[...], preferred_element_type=F32) * (1.0 / math.sqrt(FF))
        value = value.astype(BF16)
        for xa in range(X):
            for ca in range(2):
                s = xa * 2 + ca
                part[ca, xa, rows] = value[:, s * 128 : (s + 1) * 128]
        pair[i] = put(part.at[1 - c, :, rows], part_got.at[:, rows], core)

    def summed(i, k):
        xa = at_x(k)
        rows = chunk(i)
        return part[c, xa, rows].astype(F32) + part_got[xa, rows].astype(F32)

    def x_first(i):
        rows = chunk(i)
        pair[i].wait_recv()
        far, far_dev, near, near_k = (x_up, 0, x_dn, -1) if i % 2 == 0 else (x_dn, 1, x_up, 1)
        one_send[2, rows] = summed(i, 2).astype(BF16)
        two[i] = put(one_send.at[2, rows], two_got.at[rows], far)
        side_n = 1 - far_dev
        one_send[side_n, rows] = summed(i, near_k).astype(BF16)
        one_dn[i] = put(one_send.at[side_n, rows], one_got.at[side_n, rows], near)

    def x_second(i):
        rows = chunk(i)
        far, side_f, k = (x_up, 0, 1) if i % 2 == 0 else (x_dn, 1, -1)
        two[i].wait_recv()
        one_send[side_f, rows] = (summed(i, k) + two_got[rows].astype(F32)).astype(BF16)
        one_up[i] = put(one_send.at[side_f, rows], one_got.at[side_f, rows], far)

    def x_last(i):
        rows = chunk(i)
        one_dn[i].wait_recv()
        one_up[i].wait_recv()
        both = one_got[0, rows].astype(F32) + one_got[1, rows].astype(F32)
        grad[rows] = (summed(i, 0) + both).astype(BF16)

    in_pre.wait()
    gelu(0, 4)
    from_y(0)
    gelu(4, 8)
    from_y(1)
    from_below(0)
    from_above(0)
    gelu(8, 12)
    from_y(2)
    from_below(1)
    from_above(1)
    gelu(12, 16)
    from_y(3)
    from_below(2)
    from_above(2)
    terms(0)
    from_below(3)
    from_above(3)
    z_step(0, 1)
    terms(-1)
    terms(1)
    z_step(0, 2)
    for s in range(PIECES):
        from_two(s)
    z_step(-1, 1)
    z_step(1, 1)
    z_step(0, 3)
    terms(2)
    z_step(-1, 2)
    z_step(1, 2)
    in_down.wait()
    in_up.wait()
    in_moment.wait()
    in_second.wait()
    partial(0)
    z_last(0)
    z_step(2, 1)
    z_step(-1, 3)
    z_step(1, 3)
    partial(1)
    x_first(0)
    z_step(2, 2)
    z_last(-1)
    z_last(1)
    partial(2)
    x_first(1)
    x_second(0)
    z_step(2, 3)
    adam(0)
    adam(-1)
    adam(1)
    partial(3)
    x_first(2)
    x_second(1)
    x_last(0)
    z_last(2)
    partial(4)
    x_first(3)
    x_second(2)
    adam(2)
    spread(yh, "own")
    side = put(new_rows(0, yh), new_rows(0, yh), mate)
    move(new_m, moment_out.at[0])
    move(new_v, second_out.at[0])
    partial(5)
    x_first(4)
    x_second(3)
    x_last(1)
    side.wait_recv()
    spread(1 - yh, "mate")
    partial(6)
    x_first(5)
    x_second(4)
    relay(yh, "own", 1)
    partial(7)
    x_first(6)
    x_second(5)
    relay(1 - yh, "mate", 1)
    x_first(7)
    x_second(6)
    relay(yh, "own", 2)
    x_second(7)
    relay(1 - yh, "mate", 2)
    x_last(2)
    x_last(3)
    x_last(4)
    relay(yh, "own", 3)
    x_last(5)
    relay(1 - yh, "mate", 3)
    x_last(6)
    x_last(7)
    move(grad, grad_out.at[0])
    for key in ("own", "mate"):
        ring_up[key].wait_recv()
        ring_dn[key].wait_recv()
    move(fresh, down_out.at[0])
    for copy in sent:
        copy.wait_send()
    for copy in stays[5:]:
        copy.wait()


def on_device(handoff, hidden_pre, down_weight, up_weight, moment, second):
    anywhere = pl.BlockSpec(memory_space=pl.ANY)
    return pl.pallas_call(
        kernel,
        out_shape=(
            jax.ShapeDtypeStruct((1, TOK, 128), BF16),
            jax.ShapeDtypeStruct((1, HW, D), BF16),
            jax.ShapeDtypeStruct((1, ROWS, D), F32),
            jax.ShapeDtypeStruct((1, ROWS, D), F32),
        ),
        in_specs=[anywhere] * 6,
        out_specs=(anywhere,) * 4,
        scratch_shapes=[
            pltpu.VMEM((2 * X, TOK, 128), BF16),
            pltpu.VMEM((TOK, HW), BF16),
            pltpu.VMEM((HW, TOK), BF16),
            pltpu.VMEM((TOK, HW), F32),
            pltpu.VMEM((HW, D), BF16),
            pltpu.VMEM((HW, D), BF16),
            pltpu.VMEM((ROWS, D), F32),
            pltpu.VMEM((ROWS, D), F32),
            pltpu.VMEM((2, X, TOK, 128), BF16),
            pltpu.VMEM((X, TOK, 128), BF16),
            pltpu.VMEM((TOK, 128), BF16),
            pltpu.VMEM((3, TOK, 128), BF16),
            pltpu.VMEM((2, TOK, 128), BF16),
            pltpu.VMEM((TOK, 128), BF16),
            pltpu.VMEM((X, HW, COLS), BF16),
            pltpu.VMEM((X, 4, 2 * ROWS, COLS), BF16),
            pltpu.VMEM((X, 4, 2 * ROWS, COLS), BF16),
            pltpu.VMEM((X, 2 * ROWS, COLS), F32),
            pltpu.VMEM((X, 2 * ROWS, COLS), BF16),
            pltpu.VMEM((X, ROWS, COLS), BF16),
            pltpu.VMEM((ROWS, D), F32),
            pltpu.VMEM((ROWS, D), F32),
            pltpu.VMEM((HW, D), BF16),
            pltpu.SemaphoreType.DMA((N_SENDS,)),
            pltpu.SemaphoreType.DMA((N_SENDS,)),
            pltpu.SemaphoreType.DMA((16,)),
        ],
        compiler_params=pltpu.CompilerParams(
            collective_id=0, has_side_effects=True, vmem_limit_bytes=56 * 1024 * 1024
        ),
        cost_estimate=pl.CostEstimate(flops=6 * TOK * HW * D, bytes_accessed=12 << 20, transcendentals=2 * TOK * HW),
    )(handoff, hidden_pre, down_weight, up_weight, moment, second)


def solution(mesh):
    placed = (
        P("pipe", "dp", "tensor"),
        P("pipe", "dp", "tensor"),
        P("pipe", "tensor", None),
        P("pipe", "tensor", None),
        P("pipe", ("tensor", "dp"), None),
        P("pipe", ("tensor", "dp"), None),
    )
    return jax.shard_map(
        on_device,
        mesh=mesh,
        in_specs=placed,
        out_specs=(
            P("pipe", "dp", "tensor"),
            P("pipe", "tensor", None),
            P("pipe", ("tensor", "dp"), None),
            P("pipe", ("tensor", "dp"), None),
        ),
        check_vma=False,
    )
```

time: 443 us -> 87.8 us (0.20)
  waiting for transfers between devices: 402 us -> 0 us
  Pallas kernels: 0 us -> 81.5 us
  matrix products: 15.3 us -> 0 us
  between operations: 13.8 us -> 0.66 us
    reduce_scatter x1 -> x0, waiting for transfers between devices: 189 us -> none  [on_device(): lax.psum_scatter((product * grad_scale).astype(jnp.bfloat16), 'dp', scatt...]
    all_gather x2 -> x0, waiting for transfers between devices: 122 us -> none  [the longest x1 78.1 us: on_device(): new_down = lax.all_gather(fresh_rows, 'dp', axis=0, tiled=True)]
    pallas_call x0 -> x1, Pallas kernels: none -> 81.5 us  [on_device(): pl.pallas_call(kernel, out_shape=(jax.ShapeDtypeStruct((1, TOK, 128), BF1...]
    psum x1 -> x0, waiting for transfers between devices: 79.6 us -> none  [on_device(): lax.psum(partial_value.astype(jnp.bfloat16), 'tensor').astype(jnp.float32)]
    dot_general x2 -> x0, matrix products: 15.4 us -> none  [the longest x1 9.17 us: on_device(): jnp.dot(act_grad, up_weight[0], preferred_element_type=jnp.float32)]
    ppermute x1 -> x0, waiting for transfers between devices: 10.7 us -> none  [from_behind(): return lax.ppermute(block, axis, route)]
  transfers between devices with their start and end apart: 5 -> 0, of which waited for: 5 -> 0; matrix products, arithmetic and copies ran while one was open for 3% -> 0% of each run, Pallas kernels for 0% -> 0%
where the time goes in v1:
time: 87.8 us; the launch traced here: 87.6 us
  Pallas kernels  81.5 us (93%)
  local copies, waits for them, and re-layouts  5.49 us (6%)
    pallas_call x1, Pallas kernels, on_device(): pl.pallas_call(kernel, out_shape=(jax.ShapeDtypeStruct((1, TOK, 128), BF1...  81.5 us
    unnamed x8, local copies, waits for them, and re-layouts  5.49 us

profile of v1, /device:TPU:1, one launch (start us, length us, event | category | flops | bytes accessed | tf_op | source)
XLA Modules:
  0.0 87.6 jit_solution(3810758121139416005)
XLA Ops:
  0.6 81.5 %shard_map.93 = (bf16[1,2048,128]{2,1,0:T(8,128)(2,1)}, bf16[1,512,1024]{2,1,0:T(8,128)(2,1)}, f32[1,32,1024]{2,1,0:T(8,128)}, f32[1,32,1024]{2,1,0:T(8,128)}) custom-call(bf16[1,2048,128]{2,1,0:T(8,128)(2,1)} %handoff.1, bf16[1,2048,512]{2,1,0:T(8,128)(2,1)} %pre_in.1, bf16[1,512,1024]{2,1,0:T(8,128)(2,1)} %down_in.1, bf16[1,512,1024]{2,1,0:T(8,128)(2,1)} %up_in.1, ...), custom_call_target="tpu_custom_call" | custom-call | flops 6442450944 | bytes 12582912 | tf_op jit(solution)/shard_map/pallas_call | solution.py:368
  82.1 0.0 copy-start.1
  82.1 0.0 copy-start
  82.2 1.9 %copy.14 = bf16[1,2048,128]{2,1,0:T(8,128)(2,1)} copy(bf16[1,2048,128]{2,1,0:T(8,128)(2,1)} %get-tuple-element.8) | data formatting | bytes 1048576
  84.1 2.3 %copy.15 = bf16[1,512,1024]{2,1,0:T(8,128)(2,1)} copy(bf16[1,512,1024]{2,1,0:T(8,128)(2,1)} %get-tuple-element.9) | data formatting | bytes 2097152
  86.3 0.0 copy-done.1
  86.3 0.7 copy.16
  87.0 0.0 copy-done
  87.0 0.7 copy.17
Async XLA Ops:
  82.1 4.2 %copy-start.1 = (f32[1,32,1024]{2,1,0:T(8,128)S(1)}, f32[1,32,1024]{2,1,0:T(8,128)}, u32[]{:S(2)}) copy-start(f32[1,32,1024]{2,1,0:T(8,128)} %get-tuple-element.10) | copy-start | bytes 393220
  82.1 4.8 %copy-start = (f32[1,32,1024]{2,1,0:T(8,128)S(1)}, f32[1,32,1024]{2,1,0:T(8,128)}, u32[]{:S(2)}) copy-start(f32[1,32,1024]{2,1,0:T(8,128)} %get-tuple-element.11) | copy-start | bytes 393220

commit v2 on v1

v2 whole, which is shorter than its diff:
```python
import math

import jax
import jax.numpy as jnp
from jax import lax
from jax.experimental import pallas as pl
from jax.experimental.pallas import tpu as pltpu
from jax.sharding import PartitionSpec as P

F32 = jnp.float32
BF16 = jnp.bfloat16

X = 4
Z = 8
D = 1024
HW = 512
TOK = 2048
FF = 4096
TOKENS = 32768
ROWS = 32
PIECES = 8
PIECE = TOK // PIECES
CHUNKS = 8
CHUNK = TOK // CHUNKS
COLS = D // X
HALF = COLS // 2


def kernel(
    handoff, pre_in, down_in, up_in, moment_in, second_in,
    grad_out, down_out, moment_out, second_out,
    inc, pre, hidden_t, slope, down, up, moment, second,
    part, part_got, two_got, one_send, one_got, grad,
    term, agg_got, fin_got, so_far, new_m, new_v, fresh,
    y_sem, x_sem, two_sem, core_sem, pair_sem, far_sem, last_sem,
    agg_sem, fin_sem, ring_sem, row_sem, send_sem, local,
):
    p = lax.axis_index("pipe")
    d = lax.axis_index("dp")
    t = lax.axis_index("tensor")
    z, yh = lax.div(d, 2), lax.rem(d, 2)
    x, c = lax.div(t, 2), lax.rem(t, 2)

    def at_x(k):
        return lax.rem(x + (k + X), X)

    def at_z(k):
        return lax.rem(z + (k + Z), Z)

    def at_h(h):
        return 1 - yh if h else yh

    def owner(k, h):
        return (p, at_z(k) * 2 + at_h(h), t)

    across = (1 - p, d, t)
    core = (p, d, x * 2 + (1 - c))
    x_up = (p, d, at_x(1) * 2 + c)
    x_dn = (p, d, at_x(-1) * 2 + c)
    near = [(k, h) for k in (2, -2, 1, -1) for h in (1, 0)]
    partners = (across, core, x_up, x_dn, owner(0, 1)) + tuple(owner(k, h) for k, h in near)

    GATHER, TERMS, NEW, GRAD = range(4)

    def put(src, dst, device, kind, sem):
        pltpu.make_async_remote_copy(
            src_ref=src, dst_ref=dst, send_sem=send_sem.at[kind], recv_sem=sem,
            device_id=device, device_id_type=pl.DeviceIdType.MESH,
        ).start()

    def landed(ref, sem):
        pltpu.make_async_remote_copy(
            src_ref=ref, dst_ref=ref, send_sem=send_sem.at[0], recv_sem=sem,
            device_id=core, device_id_type=pl.DeviceIdType.MESH,
        ).wait_recv()

    def left(ref, kind):
        pltpu.make_async_remote_copy(
            src_ref=ref, dst_ref=ref, send_sem=send_sem.at[kind], recv_sem=row_sem.at[0],
            device_id=core, device_id_type=pl.DeviceIdType.MESH,
        ).wait_send()

    stays = []

    def move(src, dst):
        copy = pltpu.make_async_copy(src, dst, local.at[len(stays)])
        copy.start()
        stays.append(copy)
        return copy

    barrier = pltpu.get_barrier_semaphore()
    for device in partners:
        pl.semaphore_signal(barrier, inc=1, device_id=device, device_id_type=pl.DeviceIdType.MESH)
    in_pre = move(pre_in.at[0], pre)
    in_down = move(down_in.at[0], down)
    in_up = move(up_in.at[0], up)
    in_moment = move(moment_in.at[0], moment)
    in_second = move(second_in.at[0], second)
    pl.semaphore_wait(barrier, len(partners))

    def piece(s, count=1):
        return pl.ds(s * PIECE, count * PIECE)

    slot_of = {k: at_x(k) * 2 + c for k in (0, -1, 1, 2)}

    def core_group(k, s):
        if k != 2:
            return core_sem.at[abs(k)]
        return core_sem.at[2 if s < 2 else 3 if s < 6 else 4]

    def share(k, s):
        block = inc.at[slot_of[k], piece(s)]
        put(block, block, core, GATHER, core_group(k, s))

    def from_y(s):
        block = inc.at[t, piece(s)]
        landed(block, y_sem.at[s])
        put(block, block, x_up, GATHER, x_sem.at[s])
        put(block, block, x_dn, GATHER, x_sem.at[s])
        share(0, s)

    def from_x(s):
        landed(inc.at[0, piece(0, 2)], x_sem.at[s])
        share(-1, s)
        share(1, s)

    def pass_on(s):
        k, device = (-1, x_up) if s % 2 == 0 else (1, x_dn)
        block = inc.at[slot_of[k], piece(s)]
        put(block, block, device, GATHER, two_sem.at[s // 2])

    def from_two(s):
        landed(inc.at[0, piece(0, 2)], two_sem.at[s // 2])
        share(2, s)
        share(2, s + 1)

    for s in range(PIECES):
        put(handoff.at[0, piece(s)], inc.at[t, piece(s)], across, GATHER, y_sem.at[s])

    GELU = 128

    def gelu(first, last):
        def body(b, carry):
            rows = pl.ds(pl.multiple_of(b * GELU, GELU), GELU)
            a = pre[rows, :].astype(F32)
            cdf = 0.5 * (1.0 + lax.erf(a * (1.0 / math.sqrt(2.0))))
            slope[rows, :] = cdf + a * jnp.exp(-0.5 * a * a) * (1.0 / math.sqrt(2.0 * math.pi))
            hidden_t[:, rows] = (a * cdf).astype(BF16).T
            return carry

        lax.fori_loop(first, last, body, 0)

    lo, hi = pl.ds(0, HALF), pl.ds(HALF, HALF)

    def rows_of(k, h=None):
        if h is None:
            return pl.ds(pl.multiple_of(at_z(k) * 2 * ROWS, 2 * ROWS), 2 * ROWS)
        return pl.ds(pl.multiple_of((at_z(k) * 2 + at_h(h)) * ROWS, ROWS), ROWS)

    def to_owner(xa, n, k, h):
        put(term.at[xa, rows_of(k, h)], fin_got.at[xa, n], owner(k, h), TERMS, fin_sem.at[xa])

    def send_terms(xa):
        sem = agg_sem.at[xa]
        put(term.at[xa, rows_of(4), lo], agg_got.at[xa, 2, :, lo], owner(2, 0), TERMS, sem)
        put(term.at[xa, rows_of(4), hi], agg_got.at[xa, 2, :, hi], owner(-2, 0), TERMS, sem)
        put(term.at[xa, rows_of(3)], agg_got.at[xa, 0], owner(1, 0), TERMS, sem)
        put(term.at[xa, rows_of(-3)], agg_got.at[xa, 1], owner(-1, 0), TERMS, sem)
        for n, (k, h) in enumerate(near):
            if abs(k) == 1:
                to_owner(xa, n, k, h)
        to_owner(xa, 8, 0, 1)

    def terms(k):
        if k != 1:
            landed(inc.at[pl.ds(0, 1 if k == 0 else 2)], core_sem.at[abs(k)])
        xa = at_x(k)
        block = jnp.concatenate([inc[xa * 2], inc[xa * 2 + 1]], axis=1)
        product = jnp.dot(hidden_t[...], block, preferred_element_type=F32)
        term[xa] = (product * (1.0 / math.sqrt(TOKENS))).astype(BF16)
        send_terms(xa)

    def two_terms(first, last):
        landed(inc.at[0, piece(0, 4 if first == 0 else 2)], core_sem.at[3 if first == 0 else 4])
        xa = at_x(2)
        toks = piece(first, last - first)
        block = jnp.concatenate([inc[xa * 2, toks], inc[xa * 2 + 1, toks]], axis=1)
        product = jnp.dot(hidden_t[:, toks], block, preferred_element_type=F32)
        if first == 0:
            so_far[...] = product
            return
        term[xa] = ((so_far[...] + product) * (1.0 / math.sqrt(TOKENS))).astype(BF16)
        send_terms(xa)

    def aggregate(k):
        xa = at_x(k)
        landed(agg_got.at[xa], agg_sem.at[xa])
        for n, step, half in ((0, 2, lo), (1, -2, hi)):
            rows = rows_of(step)
            term[xa, rows] = (term[xa, rows].astype(F32) + agg_got[xa, n].astype(F32)).astype(BF16)
            more = term[xa, rows, half].astype(F32) + agg_got[xa, 2, :, half].astype(F32)
            term[xa, rows, half] = more.astype(BF16)
        for n, (k, h) in enumerate(near):
            if abs(k) == 2:
                to_owner(xa, n, k, h)

    def block_cols(xa):
        return pl.ds(pl.multiple_of(xa * COLS, COLS), COLS)

    def adam(k):
        xa = at_x(k)
        cols = block_cols(xa)
        own = rows_of(0, 0)
        landed(fin_got.at[xa], fin_sem.at[xa])
        gradient = term[xa, own].astype(F32)
        for n in range(9):
            gradient = gradient + fin_got[xa, n].astype(F32)
        m = 0.9 * moment[:, cols] + 0.1 * gradient
        v = 0.95 * second[:, cols] + 0.05 * gradient * gradient
        new_m[:, cols] = m
        new_v[:, cols] = v
        old = down[own, cols].astype(F32)
        fresh[xa, own] = (old - 0.2 * m / (jnp.sqrt(v) + 1e-08)).astype(BF16)
        block = fresh.at[xa, own]
        for k, h in near:
            put(block, block, owner(k, h), NEW, (row_sem if abs(k) == 1 else ring_sem).at[xa])
        put(block, block, owner(0, 1), NEW, row_sem.at[xa])

    def relay(k):
        xa = at_x(k)
        landed(fresh.at[xa, pl.ds(0, 4 * ROWS)], ring_sem.at[xa])
        half = ROWS // 2
        for k, first in ((2, 0), (-2, half)):
            for h in (1, 0):
                start = (at_z(-k) * 2 + at_h(h)) * ROWS
                part_rows = fresh.at[xa, pl.ds(pl.multiple_of(start + first, half), half)]
                put(part_rows, part_rows, owner(k, 0), NEW, row_sem.at[xa])
                block = fresh.at[xa, rows_of(-k, h)]
                put(block, block, owner(k // 2, 0), NEW, row_sem.at[xa])

    def gathered(k):
        xa = at_x(k)
        landed(fresh.at[xa, pl.ds(0, 11 * ROWS)], row_sem.at[xa])
        move(fresh.at[xa], down_out.at[0, :, block_cols(xa)])

    def chunk(i):
        return pl.ds(i * CHUNK, CHUNK)

    def partial(i):
        if i == 0:
            landed(inc.at[0, piece(0, 2)], core_sem.at[2])
        rows = chunk(i)
        block = jnp.concatenate([inc[s, rows] for s in range(2 * X)], axis=1)
        back = lax.dot_general(block, down[...], (((1,), (1,)), ((), ())), preferred_element_type=F32)
        act = (back * (1.0 / math.sqrt(D)) * slope[rows, :]).astype(BF16)
        value = jnp.dot(act, up[...], preferred_element_type=F32) * (1.0 / math.sqrt(FF))
        value = value.astype(BF16)
        for xa in range(X):
            for ca in range(2):
                s = xa * 2 + ca
                part[ca, xa, rows] = value[:, s * 128 : (s + 1) * 128]
        put(part.at[1 - c, :, rows], part_got.at[:, rows], core, GRAD, pair_sem.at[i])

    def summed(i, k):
        xa = at_x(k)
        rows = chunk(i)
        return part[c, xa, rows].astype(F32) + part_got[xa, rows].astype(F32)

    def x_first(i):
        rows = chunk(i)
        landed(part_got.at[:, rows], pair_sem.at[i])
        way, k = (x_up, -1) if i % 2 == 0 else (x_dn, 1)
        one_send[2, rows] = summed(i, 2).astype(BF16)
        put(one_send.at[2, rows], two_got.at[rows], way, GRAD, far_sem.at[i])
        way, side = (x_dn, 1) if i % 2 == 0 else (x_up, 0)
        one_send[side, rows] = summed(i, k).astype(BF16)
        put(one_send.at[side, rows], one_got.at[side, rows], way, GRAD, last_sem.at[i])

    def x_second(i):
        rows = chunk(i)
        way, side, k = (x_up, 0, 1) if i % 2 == 0 else (x_dn, 1, -1)
        landed(two_got.at[rows], far_sem.at[i])
        one_send[side, rows] = (summed(i, k) + two_got[rows].astype(F32)).astype(BF16)
        put(one_send.at[side, rows], one_got.at[side, rows], way, GRAD, last_sem.at[i])

    def x_last(i):
        rows = chunk(i)
        landed(one_got.at[:, rows], last_sem.at[i])
        both = one_got[0, rows].astype(F32) + one_got[1, rows].astype(F32)
        grad[rows] = (summed(i, 0) + both).astype(BF16)

    in_pre.wait()
    gelu(0, 16)
    for s in range(PIECES):
        from_y(s)
        if s >= 3:
            from_x(s - 3)
    for s in range(5):
        pass_on(s)
    from_x(5)
    pass_on(5)
    from_x(6)
    pass_on(6)
    from_x(7)
    pass_on(7)
    terms(0)
    from_two(0)
    terms(-1)
    from_two(2)
    in_down.wait()
    in_up.wait()
    partial(0)
    terms(1)
    from_two(4)
    aggregate(0)
    from_two(6)
    partial(1)
    two_terms(0, 6)
    x_first(0)
    aggregate(-1)
    two_terms(6, 8)
    x_first(1)
    partial(2)
    aggregate(1)
    partial(3)
    x_first(2)
    in_moment.wait()
    in_second.wait()
    adam(0)
    x_first(3)
    partial(4)
    aggregate(2)
    adam(-1)
    x_first(4)
    x_second(0)
    partial(5)
    x_second(1)
    adam(1)
    x_first(5)
    relay(0)
    partial(6)
    x_second(2)
    x_first(6)
    relay(-1)
    adam(2)
    partial(7)
    x_second(3)
    x_first(7)
    relay(1)
    x_second(4)
    x_last(0)
    gathered(0)
    move(new_m, moment_out.at[0])
    move(new_v, second_out.at[0])
    x_second(5)
    relay(2)
    x_last(1)
    gathered(-1)
    x_second(6)
    x_last(2)
    x_last(3)
    gathered(1)
    x_second(7)
    x_last(4)
    x_last(5)
    x_last(6)
    x_last(7)
    move(grad, grad_out.at[0])
    gathered(2)
    left(inc, GATHER)
    left(term.at[:, pl.ds(0, 15 * ROWS)], TERMS)
    left(fresh.at[:, pl.ds(0, 15 * ROWS)], NEW)
    left(inc.at[pl.ds(0, 7)], GRAD)
    for copy in stays[5:]:
        copy.wait()


def place(
    grad, down, moment, second, grad_out, down_out, moment_out, second_out,
    grad_here, down_here, moment_here, second_here, loads, stores,
):
    parts = []
    for a, here, b, rows, n in (
        (down, down_here, down_out, HW, 4),
        (grad, grad_here, grad_out, TOK, 2),
        (moment, moment_here, moment_out, ROWS, 1),
        (second, second_here, second_out, ROWS, 1),
    ):
        for i in range(n):
            at = pl.ds(i * (rows // n), rows // n)
            parts.append((a.at[0, at], here.at[at], b.at[0, at]))
    first = [pltpu.make_async_copy(a, here, loads.at[i]) for i, (a, here, _) in enumerate(parts)]
    then = [pltpu.make_async_copy(here, b, stores.at[i]) for i, (_, here, b) in enumerate(parts)]
    for copy in first:
        copy.start()
    for load, store in zip(first, then, strict=True):
        load.wait()
        store.start()
    for copy in then:
        copy.wait()


def on_device(handoff, hidden_pre, down_weight, up_weight, moment, second):
    anywhere = pl.BlockSpec(memory_space=pl.ANY)
    shapes = (
        jax.ShapeDtypeStruct((1, TOK, 128), BF16),
        jax.ShapeDtypeStruct((1, HW, D), BF16),
        jax.ShapeDtypeStruct((1, ROWS, D), F32),
        jax.ShapeDtypeStruct((1, ROWS, D), F32),
    )
    results = pl.pallas_call(
        kernel,
        out_shape=shapes,
        in_specs=[anywhere] * 6,
        out_specs=(anywhere,) * 4,
        scratch_shapes=[
            pltpu.VMEM((2 * X, TOK, 128), BF16),
            pltpu.VMEM((TOK, HW), BF16),
            pltpu.VMEM((HW, TOK), BF16),
            pltpu.VMEM((TOK, HW), F32),
            pltpu.VMEM((HW, D), BF16),
            pltpu.VMEM((HW, D), BF16),
            pltpu.VMEM((ROWS, D), F32),
            pltpu.VMEM((ROWS, D), F32),
            pltpu.VMEM((2, X, TOK, 128), BF16),
            pltpu.VMEM((X, TOK, 128), BF16),
            pltpu.VMEM((TOK, 128), BF16),
            pltpu.VMEM((3, TOK, 128), BF16),
            pltpu.VMEM((2, TOK, 128), BF16),
            pltpu.VMEM((TOK, 128), BF16),
            pltpu.VMEM((X, HW, COLS), BF16),
            pltpu.VMEM((X, 3, 2 * ROWS, COLS), BF16),
            pltpu.VMEM((X, 9, ROWS, COLS), BF16),
            pltpu.VMEM((HW, COLS), F32),
            pltpu.VMEM((ROWS, D), F32),
            pltpu.VMEM((ROWS, D), F32),
            pltpu.VMEM((X, HW, COLS), BF16),
            pltpu.SemaphoreType.DMA((PIECES,)),
            pltpu.SemaphoreType.DMA((PIECES,)),
            pltpu.SemaphoreType.DMA((PIECES // 2,)),
            pltpu.SemaphoreType.DMA((5,)),
            pltpu.SemaphoreType.DMA((CHUNKS,)),
            pltpu.SemaphoreType.DMA((CHUNKS,)),
            pltpu.SemaphoreType.DMA((CHUNKS,)),
            pltpu.SemaphoreType.DMA((X,)),
            pltpu.SemaphoreType.DMA((X,)),
            pltpu.SemaphoreType.DMA((X,)),
            pltpu.SemaphoreType.DMA((X,)),
            pltpu.SemaphoreType.DMA((4,)),
            pltpu.SemaphoreType.DMA((12,)),
        ],
        compiler_params=pltpu.CompilerParams(
            collective_id=0, has_side_effects=True, vmem_limit_bytes=56 * 1024 * 1024
        ),
        cost_estimate=pl.CostEstimate(flops=6 * TOK * HW * D, bytes_accessed=12 << 20, transcendentals=2 * TOK * HW),
    )(handoff, hidden_pre, down_weight, up_weight, moment, second)
    return pl.pallas_call(
        place,
        out_shape=shapes,
        in_specs=[anywhere] * 4,
        out_specs=(anywhere,) * 4,
        scratch_shapes=[
            pltpu.VMEM((TOK, 128), BF16),
            pltpu.VMEM((HW, D), BF16),
            pltpu.VMEM((ROWS, D), F32),
            pltpu.VMEM((ROWS, D), F32),
            pltpu.SemaphoreType.DMA((8,)),
            pltpu.SemaphoreType.DMA((8,)),
        ],
    )(*results)


def solution(mesh):
    placed = (
        P("pipe", "dp", "tensor"),
        P("pipe", "dp", "tensor"),
        P("pipe", "tensor", None),
        P("pipe", "tensor", None),
        P("pipe", ("tensor", "dp"), None),
        P("pipe", ("tensor", "dp"), None),
    )
    return jax.shard_map(
        on_device,
        mesh=mesh,
        in_specs=placed,
        out_specs=(
            P("pipe", "dp", "tensor"),
            P("pipe", "tensor", None),
            P("pipe", ("tensor", "dp"), None),
            P("pipe", ("tensor", "dp"), None),
        ),
        check_vma=False,
    )
```

time: 87.8 us -> 65.7 us (0.75)
  Pallas kernels: 81.5 us -> 64.4 us
  local copies, waits for them, and re-layouts: 5.49 us -> 0 us
    pallas_call x1 -> x2, Pallas kernels: 81.5 us -> 64.4 us  [the longest x1 62.1 us: on_device(): pl.pallas_call(kernel, out_shape=shapes, in_specs=[anywhere] * 6, out_spe...]
    unnamed x8 -> x0, local copies, waits for them, and re-layouts: 5.49 us -> none
where the time goes in v2:
time: 65.7 us; the launch traced here: 65 us
  Pallas kernels  64.4 us (98%)
    pallas_call x1, Pallas kernels, on_device(): pl.pallas_call(kernel, out_shape=shapes, in_specs=[anywhere] * 6, out_spe...  62.1 us
    pallas_call x1, Pallas kernels, on_device(): pl.pallas_call(place, out_shape=shapes, in_specs=[anywhere] * 4, out_spec...  2.31 us

profile of v2, /device:TPU:1, one launch (start us, length us, event | category | flops | bytes accessed | tf_op | source)
XLA Modules:
  0.0 65.0 jit_solution(444910693621474719)
XLA Ops:
  0.6 62.1 %shard_map.93 = (bf16[1,2048,128]{2,1,0:T(8,128)(2,1)}, bf16[1,512,1024]{2,1,0:T(8,128)(2,1)}, f32[1,32,1024]{2,1,0:T(8,128)}, f32[1,32,1024]{2,1,0:T(8,128)}) custom-call(bf16[1,2048,128]{2,1,0:T(8,128)(2,1)} %handoff.1, bf16[1,2048,512]{2,1,0:T(8,128)(2,1)} %pre_in.1, bf16[1,512,1024]{2,1,0:T(8,128)(2,1)} %down_in.1, bf16[1,512,1024]{2,1,0:T(8,128)(2,1)} %up_in.1, ...), custom_call_target="tpu_custom_call" | custom-call | flops 6442450944 | bytes 12582912 | tf_op jit(solution)/shard_map/pallas_call | solution.py:411
  62.7 2.3 %shard_map.94 = (bf16[1,2048,128]{2,1,0:T(8,128)(2,1)}, bf16[1,512,1024]{2,1,0:T(8,128)(2,1)}, f32[1,32,1024]{2,1,0:T(8,128)}, f32[1,32,1024]{2,1,0:T(8,128)}) custom-call(bf16[1,2048,128]{2,1,0:T(8,128)(2,1)} %get-tuple-element.8.grad, bf16[1,512,1024]{2,1,0:T(8,128)(2,1)} %get-tuple-element.9.down, f32[1,32,1024]{2,1,0:T(8,128)} %get-tuple-element.10.moment, ...), custom_call_target="tpu_custom_call" | custom-call | tf_op jit(solution)/shard_map/pallas_call | solution.py:457

commit v3 on v2

--- a/solution.py
+++ b/solution.py
@@ -18,8 +18,9 @@
 FF = 4096
 TOKENS = 32768
 ROWS = 32
-PIECES = 8
-PIECE = TOK // PIECES
+SIZES = (128, 128, 256, 256, 256, 256, 256, 256, 128, 128)
+PIECES = len(SIZES)
+EARLY = 6
 CHUNKS = 8
 CHUNK = TOK // CHUNKS
 COLS = D // X
@@ -28,10 +29,10 @@
 
 def kernel(
     handoff, pre_in, down_in, up_in, moment_in, second_in,
-    grad_out, down_out, moment_out, second_out,
+    grad, fresh, new_m, new_v,
     inc, pre, hidden_t, slope, down, up, moment, second,
-    part, part_got, two_got, one_send, one_got, grad,
-    term, agg_got, fin_got, so_far, new_m, new_v, fresh,
+    part, part_got, two_got, one_send, one_got,
+    term, agg_got, fin_got, so_far,
     y_sem, x_sem, two_sem, core_sem, pair_sem, far_sem, last_sem,
     agg_sem, fin_sem, ring_sem, row_sem, send_sem, local,
 ):
@@ -57,8 +58,10 @@
     core = (p, d, x * 2 + (1 - c))
     x_up = (p, d, at_x(1) * 2 + c)
     x_dn = (p, d, at_x(-1) * 2 + c)
+    x_up_too = (p, d, at_x(1) * 2 + (1 - c))
+    x_dn_too = (p, d, at_x(-1) * 2 + (1 - c))
     near = [(k, h) for k in (2, -2, 1, -1) for h in (1, 0)]
-    partners = (across, core, x_up, x_dn, owner(0, 1)) + tuple(owner(k, h) for k, h in near)
+    partners = (across, core, x_up, x_dn, x_up_too, x_dn_too, owner(0, 1)) + tuple(owner(k, h) for k, h in near)
 
     GATHER, TERMS, NEW, GRAD = range(4)
 
@@ -99,18 +102,28 @@
     pl.semaphore_wait(barrier, len(partners))
 
     def piece(s, count=1):
-        return pl.ds(s * PIECE, count * PIECE)
+        return pl.ds(sum(SIZES[:s]), sum(SIZES[s : s + count]))
+
+    def tokens(n):
+        return pl.ds(0, n)
 
     slot_of = {k: at_x(k) * 2 + c for k in (0, -1, 1, 2)}
 
     def core_group(k, s):
-        if k != 2:
-            return core_sem.at[abs(k)]
-        return core_sem.at[2 if s < 2 else 3 if s < 6 else 4]
+        if k == 2:
+            return 4 + s // 2
+        return 2 * abs(k) + (0 if s < EARLY else 1)
+
+    def from_core(group):
+        if group >= 4:
+            landed(inc.at[0, piece(2 * group - 8, 2)], core_sem.at[group])
+        else:
+            toks = piece(0, EARLY) if group % 2 == 0 else piece(EARLY, PIECES - EARLY)
+            landed(inc.at[pl.ds(0, 1 + group // 2), toks], core_sem.at[group])
 
     def share(k, s):
         block = inc.at[slot_of[k], piece(s)]
-        put(block, block, core, GATHER, core_group(k, s))
+        put(block, block, core, GATHER, core_sem.at[core_group(k, s)])
 
     def from_y(s):
         block = inc.at[t, piece(s)]
@@ -120,7 +133,7 @@
         share(0, s)
 
     def from_x(s):
-        landed(inc.at[0, piece(0, 2)], x_sem.at[s])
+        landed(inc.at[0, tokens(2 * SIZES[s])], x_sem.at[s])
         share(-1, s)
         share(1, s)
 
@@ -128,9 +141,14 @@
         k, device = (-1, x_up) if s % 2 == 0 else (1, x_dn)
         block = inc.at[slot_of[k], piece(s)]
         put(block, block, device, GATHER, two_sem.at[s // 2])
+        if s >= PIECES - 2:
+            put(block, block, x_up_too if s % 2 == 0 else x_dn_too, GATHER, two_sem.at[s // 2])
 
     def from_two(s):
-        landed(inc.at[0, piece(0, 2)], two_sem.at[s // 2])
+        if s == PIECES - 2:
+            landed(inc.at[0, tokens(4 * SIZES[s])], two_sem.at[s // 2])
+            return
+        landed(inc.at[0, tokens(2 * SIZES[s])], two_sem.at[s // 2])
         share(2, s)
         share(2, s + 1)
 
@@ -171,25 +189,15 @@
                 to_owner(xa, n, k, h)
         to_owner(xa, 8, 0, 1)
 
-    def terms(k):
-        if k != 1:
-            landed(inc.at[pl.ds(0, 1 if k == 0 else 2)], core_sem.at[abs(k)])
-        xa = at_x(k)
-        block = jnp.concatenate([inc[xa * 2], inc[xa * 2 + 1]], axis=1)
-        product = jnp.dot(hidden_t[...], block, preferred_element_type=F32)
-        term[xa] = (product * (1.0 / math.sqrt(TOKENS))).astype(BF16)
-        send_terms(xa)
-
-    def two_terms(first, last):
-        landed(inc.at[0, piece(0, 4 if first == 0 else 2)], core_sem.at[3 if first == 0 else 4])
-        xa = at_x(2)
-        toks = piece(first, last - first)
+    def terms(k, first):
+        xa = at_x(k)
+        toks = piece(0, EARLY) if first else piece(EARLY, PIECES - EARLY)
         block = jnp.concatenate([inc[xa * 2, toks], inc[xa * 2 + 1, toks]], axis=1)
         product = jnp.dot(hidden_t[:, toks], block, preferred_element_type=F32)
-        if first == 0:
-            so_far[...] = product
+        if first:
+            so_far[k + 1] = product
             return
-        term[xa] = ((so_far[...] + product) * (1.0 / math.sqrt(TOKENS))).astype(BF16)
+        term[xa] = ((so_far[k + 1] + product) * (1.0 / math.sqrt(TOKENS))).astype(BF16)
         send_terms(xa)
 
     def aggregate(k):
@@ -241,14 +249,11 @@
     def gathered(k):
         xa = at_x(k)
         landed(fresh.at[xa, pl.ds(0, 11 * ROWS)], row_sem.at[xa])
-        move(fresh.at[xa], down_out.at[0, :, block_cols(xa)])
 
     def chunk(i):
         return pl.ds(i * CHUNK, CHUNK)
 
     def partial(i):
-        if i == 0:
-            landed(inc.at[0, piece(0, 2)], core_sem.at[2])
         rows = chunk(i)
         block = jnp.concatenate([inc[s, rows] for s in range(2 * X)], axis=1)
         back = lax.dot_general(block, down[...], (((1,), (1,)), ((), ())), preferred_element_type=F32)
@@ -291,112 +296,107 @@
 
     in_pre.wait()
     gelu(0, 16)
-    for s in range(PIECES):
+    for s in range(PIECES - 1):
         from_y(s)
         if s >= 3:
             from_x(s - 3)
-    for s in range(5):
+    from_y(9)
+    for s in range(6):
         pass_on(s)
-    from_x(5)
-    pass_on(5)
     from_x(6)
     pass_on(6)
+    from_core(0)
+    terms(0, True)
     from_x(7)
     pass_on(7)
-    terms(0)
+    from_x(8)
+    pass_on(8)
+    from_core(1)
+    terms(0, False)
+    from_x(9)
+    pass_on(9)
     from_two(0)
-    terms(-1)
+    from_core(2)
+    terms(-1, True)
     from_two(2)
+    terms(1, True)
+    from_core(3)
+    terms(-1, False)
+    from_two(4)
+    terms(1, False)
     in_down.wait()
     in_up.wait()
+    from_core(4)
     partial(0)
-    terms(1)
-    from_two(4)
+    from_two(6)
     aggregate(0)
-    from_two(6)
+    from_core(5)
     partial(1)
-    two_terms(0, 6)
+    from_core(6)
+    terms(2, True)
+    from_two(8)
+    from_core(7)
+    terms(2, False)
     x_first(0)
     aggregate(-1)
-    two_terms(6, 8)
+    partial(2)
     x_first(1)
-    partial(2)
     aggregate(1)
     partial(3)
+    partial(4)
     x_first(2)
+    partial(5)
+    x_first(3)
+    partial(6)
+    aggregate(2)
+    x_first(4)
+    partial(7)
+    x_first(5)
     in_moment.wait()
     in_second.wait()
     adam(0)
-    x_first(3)
-    partial(4)
-    aggregate(2)
+    x_second(0)
+    x_first(6)
+    x_second(1)
     adam(-1)
-    x_first(4)
-    x_second(0)
-    partial(5)
-    x_second(1)
+    x_first(7)
+    x_second(2)
     adam(1)
-    x_first(5)
+    x_second(3)
+    adam(2)
     relay(0)
-    partial(6)
-    x_second(2)
-    x_first(6)
+    x_second(4)
     relay(-1)
-    adam(2)
-    partial(7)
-    x_second(3)
-    x_first(7)
+    x_last(0)
+    x_second(5)
     relay(1)
-    x_second(4)
-    x_last(0)
+    x_last(1)
+    x_second(6)
+    relay(2)
     gathered(0)
-    move(new_m, moment_out.at[0])
-    move(new_v, second_out.at[0])
-    x_second(5)
-    relay(2)
-    x_last(1)
-    gathered(-1)
-    x_second(6)
     x_last(2)
     x_last(3)
-    gathered(1)
     x_second(7)
+    gathered(-1)
     x_last(4)
     x_last(5)
+    gathered(1)
     x_last(6)
     x_last(7)
-    move(grad, grad_out.at[0])
     gathered(2)
     left(inc, GATHER)
     left(term.at[:, pl.ds(0, 15 * ROWS)], TERMS)
     left(fresh.at[:, pl.ds(0, 15 * ROWS)], NEW)
     left(inc.at[pl.ds(0, 7)], GRAD)
-    for copy in stays[5:]:
-        copy.wait()
-
-
-def place(
-    grad, down, moment, second, grad_out, down_out, moment_out, second_out,
-    grad_here, down_here, moment_here, second_here, loads, stores,
-):
-    parts = []
-    for a, here, b, rows, n in (
-        (down, down_here, down_out, HW, 4),
-        (grad, grad_here, grad_out, TOK, 2),
-        (moment, moment_here, moment_out, ROWS, 1),
-        (second, second_here, second_out, ROWS, 1),
-    ):
-        for i in range(n):
-            at = pl.ds(i * (rows // n), rows // n)
-            parts.append((a.at[0, at], here.at[at], b.at[0, at]))
-    first = [pltpu.make_async_copy(a, here, loads.at[i]) for i, (a, here, _) in enumerate(parts)]
-    then = [pltpu.make_async_copy(here, b, stores.at[i]) for i, (_, here, b) in enumerate(parts)]
-    for copy in first:
+
+
+def place(grad, fresh, moment, second, grad_out, down_out, moment_out, second_out, sems):
+    pairs = [(grad, grad_out.at[0]), (moment, moment_out.at[0]), (second, second_out.at[0])]
+    pairs += [(fresh.at[i], down_out.at[0, :, pl.ds(i * COLS, COLS)]) for i in range(X)]
+    copies = [pltpu.make_async_copy(a, b, sems.at[i]) for i, (a, b) in enumerate(pairs)]
+    for copy in copies:
         copy.start()
-    for load, store in zip(first, then, strict=True):
-        load.wait()
-        store.start()
-    for copy in then:
+    for copy in copies:
         copy.wait()
 
 
@@ -410,9 +410,14 @@
     )
     results = pl.pallas_call(
         kernel,
-        out_shape=shapes,
+        out_shape=(
+            pltpu.VMEM((TOK, 128), BF16),
+            pltpu.VMEM((X, HW, COLS), BF16),
+            pltpu.VMEM((ROWS, D), F32),
+            pltpu.VMEM((ROWS, D), F32),
+        ),
         in_specs=[anywhere] * 6,
-        out_specs=(anywhere,) * 4,
+        out_specs=(pl.BlockSpec(memory_space=pltpu.VMEM),) * 4,
         scratch_shapes=[
             pltpu.VMEM((2 * X, TOK, 128), BF16),
             pltpu.VMEM((TOK, HW), BF16),
@@ -427,18 +432,14 @@
             pltpu.VMEM((TOK, 128), BF16),
             pltpu.VMEM((3, TOK, 128), BF16),
             pltpu.VMEM((2, TOK, 128), BF16),
-            pltpu.VMEM((TOK, 128), BF16),
             pltpu.VMEM((X, HW, COLS), BF16),
             pltpu.VMEM((X, 3, 2 * ROWS, COLS), BF16),
             pltpu.VMEM((X, 9, ROWS, COLS), BF16),
-            pltpu.VMEM((HW, COLS), F32),
-            pltpu.VMEM((ROWS, D), F32),
-            pltpu.VMEM((ROWS, D), F32),
-            pltpu.VMEM((X, HW, COLS), BF16),
+            pltpu.VMEM((X, HW, COLS), F32),
             pltpu.SemaphoreType.DMA((PIECES,)),
             pltpu.SemaphoreType.DMA((PIECES,)),
             pltpu.SemaphoreType.DMA((PIECES // 2,)),
-            pltpu.SemaphoreType.DMA((5,)),
+            pltpu.SemaphoreType.DMA((8,)),
             pltpu.SemaphoreType.DMA((CHUNKS,)),
             pltpu.SemaphoreType.DMA((CHUNKS,)),
             pltpu.SemaphoreType.DMA((CHUNKS,)),
@@ -447,7 +448,7 @@
             pltpu.SemaphoreType.DMA((X,)),
             pltpu.SemaphoreType.DMA((X,)),
             pltpu.SemaphoreType.DMA((4,)),
-            pltpu.SemaphoreType.DMA((12,)),
+            pltpu.SemaphoreType.DMA((5,)),
         ],
         compiler_params=pltpu.CompilerParams(
             collective_id=0, has_side_effects=True, vmem_limit_bytes=56 * 1024 * 1024
@@ -457,17 +458,10 @@
     return pl.pallas_call(
         place,
         out_shape=shapes,
-        in_specs=[anywhere] * 4,
+        in_specs=[pl.BlockSpec(memory_space=pltpu.VMEM)] * 4,
         out_specs=(anywhere,) * 4,
-        scratch_shapes=[
-            pltpu.VMEM((TOK, 128), BF16),
-            pltpu.VMEM((HW, D), BF16),
-            pltpu.VMEM((ROWS, D), F32),
-            pltpu.VMEM((ROWS, D), F32),
-            pltpu.SemaphoreType.DMA((8,)),
-            pltpu.SemaphoreType.DMA((8,)),
-        ],
-    )(*results)
+        scratch_shapes=[pltpu.SemaphoreType.DMA((7,))],
+    )(*(pltpu.with_memory_space_constraint(r, pltpu.VMEM) for r in results))
 
 
 def solution(mesh):

time: 65.7 us -> 62.6 us (0.953)
  Pallas kernels: 64.4 us -> 61.9 us
    pallas_call x2, Pallas kernels: 64.4 us -> 61.9 us  [the longest x1 60.6 us: on_device(): pl.pallas_call(kernel, out_shape=(pltpu.VMEM((TOK, 128), BF16), pltpu.VME...]
where the time goes in v3:
time: 62.6 us; the launch traced here: 62.5 us
  Pallas kernels  61.9 us (99%)
  between operations  0.64 us (1%)
    pallas_call x1, Pallas kernels, on_device(): pl.pallas_call(kernel, out_shape=(pltpu.VMEM((TOK, 128), BF16), pltpu.VME...  60.6 us
    pallas_call x1, Pallas kernels, on_device(): pl.pallas_call(place, out_shape=shapes, in_specs=[pl.BlockSpec(memory_spa...  1.28 us

profile of v3, /device:TPU:1, one launch (start us, length us, event | category | flops | bytes accessed | tf_op | source)
XLA Modules:
  0.0 62.5 jit_solution(16479761060790375245)
XLA Ops:
  0.6 60.6 %shard_map.93 = (bf16[2048,128]{1,0:T(8,128)(2,1)S(1)}, bf16[4,512,256]{2,1,0:T(8,128)(2,1)S(1)}, f32[32,1024]{1,0:T(8,128)S(1)}, f32[32,1024]{1,0:T(8,128)S(1)}) custom-call(bf16[1,2048,128]{2,1,0:T(8,128)(2,1)} %handoff.1, bf16[1,2048,512]{2,1,0:T(8,128)(2,1)} %pre_in.1, bf16[1,512,1024]{2,1,0:T(8,128)(2,1)} %down_in.1, bf16[1,512,1024]{2,1,0:T(8,128)(2,1)} %up_in.1, ...), custom_call_target="tpu_custom_call" | custom-call | flops 6442450944 | bytes 12582912 | tf_op jit(solution)/shard_map/pallas_call | solution.py:411
  61.3 1.3 %shard_map.94 = (bf16[1,2048,128]{2,1,0:T(8,128)(2,1)}, bf16[1,512,1024]{2,1,0:T(8,128)(2,1)}, f32[1,32,1024]{2,1,0:T(8,128)}, f32[1,32,1024]{2,1,0:T(8,128)}) custom-call(bf16[2048,128]{1,0:T(8,128)(2,1)S(1)} %get-tuple-element.8.grad, bf16[4,512,256]{2,1,0:T(8,128)(2,1)S(1)} %get-tuple-element.9.fresh, f32[32,1024]{1,0:T(8,128)S(1)} %get-tuple-element.10.moment, ...), custom_call_target="tpu_custom_call" | custom-call | tf_op jit(solution)/shard_map/pallas_call | solution.py:458

commit v4 on v3

--- a/solution.py
+++ b/solution.py
@@ -30,7 +30,7 @@
 def kernel(
     handoff, pre_in, down_in, up_in, moment_in, second_in,
     grad, fresh, new_m, new_v,
-    inc, pre, hidden_t, slope, down, up, moment, second,
+    inc, hand_here, pre, hidden_t, slope, down, up, moment, second,
     part, part_got, two_got, one_send, one_got,
     term, agg_got, fin_got, so_far,
     y_sem, x_sem, two_sem, core_sem, pair_sem, far_sem, last_sem,
@@ -61,6 +61,7 @@
     x_up_too = (p, d, at_x(1) * 2 + (1 - c))
     x_dn_too = (p, d, at_x(-1) * 2 + (1 - c))
     near = [(k, h) for k in (2, -2, 1, -1) for h in (1, 0)]
+    beside = near[4:]
     partners = (across, core, x_up, x_dn, x_up_too, x_dn_too, owner(0, 1)) + tuple(owner(k, h) for k, h in near)
 
     GATHER, TERMS, NEW, GRAD = range(4)
@@ -94,11 +95,9 @@
     barrier = pltpu.get_barrier_semaphore()
     for device in partners:
         pl.semaphore_signal(barrier, inc=1, device_id=device, device_id_type=pl.DeviceIdType.MESH)
+    in_hand = move(handoff.at[0], hand_here)
     in_pre = move(pre_in.at[0], pre)
-    in_down = move(down_in.at[0], down)
-    in_up = move(up_in.at[0], up)
-    in_moment = move(moment_in.at[0], moment)
-    in_second = move(second_in.at[0], second)
+    in_hand.wait()
     pl.semaphore_wait(barrier, len(partners))
 
     def piece(s, count=1):
@@ -153,7 +152,11 @@
         share(2, s + 1)
 
     for s in range(PIECES):
-        put(handoff.at[0, piece(s)], inc.at[t, piece(s)], across, GATHER, y_sem.at[s])
+        put(hand_here.at[piece(s)], inc.at[t, piece(s)], across, GATHER, y_sem.at[s])
+    in_down = move(down_in.at[0], down)
+    in_up = move(up_in.at[0], up)
+    in_moment = move(moment_in.at[0], moment)
+    in_second = move(second_in.at[0], second)
 
     GELU = 128
 
@@ -170,24 +173,26 @@
 
     lo, hi = pl.ds(0, HALF), pl.ds(HALF, HALF)
 
-    def rows_of(k, h=None):
-        if h is None:
-            return pl.ds(pl.multiple_of(at_z(k) * 2 * ROWS, 2 * ROWS), 2 * ROWS)
+    def rows_of(k, h):
         return pl.ds(pl.multiple_of((at_z(k) * 2 + at_h(h)) * ROWS, ROWS), ROWS)
 
-    def to_owner(xa, n, k, h):
-        put(term.at[xa, rows_of(k, h)], fin_got.at[xa, n], owner(k, h), TERMS, fin_sem.at[xa])
-
-    def send_terms(xa):
+    def send_far(k):
+        xa = at_x(k)
         sem = agg_sem.at[xa]
-        put(term.at[xa, rows_of(4), lo], agg_got.at[xa, 2, :, lo], owner(2, 0), TERMS, sem)
-        put(term.at[xa, rows_of(4), hi], agg_got.at[xa, 2, :, hi], owner(-2, 0), TERMS, sem)
-        put(term.at[xa, rows_of(3)], agg_got.at[xa, 0], owner(1, 0), TERMS, sem)
-        put(term.at[xa, rows_of(-3)], agg_got.at[xa, 1], owner(-1, 0), TERMS, sem)
-        for n, (k, h) in enumerate(near):
-            if abs(k) == 1:
-                to_owner(xa, n, k, h)
-        to_owner(xa, 8, 0, 1)
+        for h in (1, 0):
+            rows = rows_of(4, h)
+            put(term.at[xa, rows, lo], agg_got.at[xa, 6 + h, :, lo], owner(2, h), TERMS, sem)
+            put(term.at[xa, rows, hi], agg_got.at[xa, 6 + h, :, hi], owner(-2, h), TERMS, sem)
+        for n, step in enumerate((1, -1)):
+            for h in (1, 0):
+                put(term.at[xa, rows_of(3 * step, h)], agg_got.at[xa, 2 * n + h], owner(step, h), TERMS, sem)
+            put(term.at[xa, rows_of(2 * step, 1)], agg_got.at[xa, 4 + n], owner(0, 1), TERMS, sem)
+
+    def send_near(k):
+        xa = at_x(k)
+        for n, (step, h) in enumerate(beside):
+            put(term.at[xa, rows_of(step, h)], fin_got.at[xa, n], owner(step, h), TERMS, fin_sem.at[xa])
+        put(term.at[xa, rows_of(0, 1)], fin_got.at[xa, 4], owner(0, 1), TERMS, fin_sem.at[xa])
 
     def terms(k, first):
         xa = at_x(k)
@@ -198,19 +203,21 @@
             so_far[k + 1] = product
             return
         term[xa] = ((so_far[k + 1] + product) * (1.0 / math.sqrt(TOKENS))).astype(BF16)
-        send_terms(xa)
+        send_far(k)
 
     def aggregate(k):
         xa = at_x(k)
         landed(agg_got.at[xa], agg_sem.at[xa])
-        for n, step, half in ((0, 2, lo), (1, -2, hi)):
-            rows = rows_of(step)
-            term[xa, rows] = (term[xa, rows].astype(F32) + agg_got[xa, n].astype(F32)).astype(BF16)
-            more = term[xa, rows, half].astype(F32) + agg_got[xa, 2, :, half].astype(F32)
-            term[xa, rows, half] = more.astype(BF16)
-        for n, (k, h) in enumerate(near):
-            if abs(k) == 2:
-                to_owner(xa, n, k, h)
+        for n, step in enumerate((2, -2)):
+            rows = rows_of(step, 0)
+            mine = term[xa, rows].astype(F32) + agg_got[xa, 4 + n].astype(F32)
+            mine = mine + (agg_got[xa, 2 * n].astype(F32) + agg_got[xa, 2 * n + 1].astype(F32))
+            side = slice(0, HALF) if n == 0 else slice(HALF, COLS)
+            more = agg_got[xa, 6, :, side].astype(F32) + agg_got[xa, 7, :, side].astype(F32)
+            whole = [mine[:, :HALF], mine[:, HALF:]]
+            whole[n] = whole[n] + more
+            term[xa, rows] = jnp.concatenate(whole, axis=1).astype(BF16)
+            put(term.at[xa, rows], fin_got.at[xa, 5 + n], owner(step, 0), TERMS, fin_sem.at[xa])
 
     def block_cols(xa):
         return pl.ds(pl.multiple_of(xa * COLS, COLS), COLS)
@@ -221,7 +228,7 @@
         own = rows_of(0, 0)
         landed(fin_got.at[xa], fin_sem.at[xa])
         gradient = term[xa, own].astype(F32)
-        for n in range(9):
+        for n in range(7):
             gradient = gradient + fin_got[xa, n].astype(F32)
         m = 0.9 * moment[:, cols] + 0.1 * gradient
         v = 0.95 * second[:, cols] + 0.05 * gradient * gradient
@@ -230,25 +237,29 @@
         old = down[own, cols].astype(F32)
         fresh[xa, own] = (old - 0.2 * m / (jnp.sqrt(v) + 1e-08)).astype(BF16)
         block = fresh.at[xa, own]
-        for k, h in near:
-            put(block, block, owner(k, h), NEW, (row_sem if abs(k) == 1 else ring_sem).at[xa])
+        for step in (2, -2):
+            put(block, block, owner(step, 0), NEW, ring_sem.at[xa])
+        for step, h in beside:
+            put(block, block, owner(step, h), NEW, row_sem.at[xa])
         put(block, block, owner(0, 1), NEW, row_sem.at[xa])
 
     def relay(k):
         xa = at_x(k)
-        landed(fresh.at[xa, pl.ds(0, 4 * ROWS)], ring_sem.at[xa])
+        landed(fresh.at[xa, pl.ds(0, 2 * ROWS)], ring_sem.at[xa])
         half = ROWS // 2
-        for k, first in ((2, 0), (-2, half)):
+        for step, first in ((1, 0), (-1, half)):
+            block = fresh.at[xa, rows_of(-2 * step, 0)]
+            start = (at_z(-2 * step) * 2 + yh) * ROWS + first
+            part_rows = fresh.at[xa, pl.ds(pl.multiple_of(start, half), half)]
             for h in (1, 0):
-                start = (at_z(-k) * 2 + at_h(h)) * ROWS
-                part_rows = fresh.at[xa, pl.ds(pl.multiple_of(start + first, half), half)]
-                put(part_rows, part_rows, owner(k, 0), NEW, row_sem.at[xa])
-                block = fresh.at[xa, rows_of(-k, h)]
-                put(block, block, owner(k // 2, 0), NEW, row_sem.at[xa])
+                put(part_rows, part_rows, owner(2 * step, h), NEW, row_sem.at[xa])
+            for h in (1, 0):
+                put(block, block, owner(step, h), NEW, row_sem.at[xa])
+            put(block, block, owner(0, 1), NEW, row_sem.at[xa])
 
     def gathered(k):
         xa = at_x(k)
-        landed(fresh.at[xa, pl.ds(0, 11 * ROWS)], row_sem.at[xa])
+        landed(fresh.at[xa, pl.ds(0, 13 * ROWS)], row_sem.at[xa])
 
     def chunk(i):
         return pl.ds(i * CHUNK, CHUNK)
@@ -294,39 +305,57 @@
         both = one_got[0, rows].astype(F32) + one_got[1, rows].astype(F32)
         grad[rows] = (summed(i, 0) + both).astype(BF16)
 
+    from_y(0)
     in_pre.wait()
-    gelu(0, 16)
-    for s in range(PIECES - 1):
-        from_y(s)
-        if s >= 3:
-            from_x(s - 3)
+    gelu(0, 2)
+    from_y(1)
+    gelu(2, 6)
+    from_y(2)
+    gelu(6, 10)
+    from_y(3)
+    from_x(0)
+    gelu(10, 14)
+    from_y(4)
+    from_x(1)
+    gelu(14, 16)
+    from_y(5)
+    from_x(2)
+    from_y(6)
+    from_x(3)
+    from_y(7)
+    from_x(4)
+    from_y(8)
+    from_x(5)
     from_y(9)
     for s in range(6):
         pass_on(s)
+    from_core(0)
+    terms(0, True)
     from_x(6)
     pass_on(6)
-    from_core(0)
-    terms(0, True)
+    from_core(2)
+    terms(-1, True)
     from_x(7)
     pass_on(7)
+    from_core(1)
+    terms(0, False)
+    send_near(0)
     from_x(8)
     pass_on(8)
-    from_core(1)
-    terms(0, False)
     from_x(9)
     pass_on(9)
-    from_two(0)
-    from_core(2)
-    terms(-1, True)
-    from_two(2)
     terms(1, True)
     from_core(3)
     terms(-1, False)
-    from_two(4)
+    from_two(0)
+    from_two(2)
     terms(1, False)
+    send_near(-1)
+    send_near(1)
     in_down.wait()
     in_up.wait()
     from_core(4)
+    from_two(4)
     partial(0)
     from_two(6)
     aggregate(0)
@@ -334,56 +363,57 @@
     partial(1)
     from_core(6)
     terms(2, True)
+    x_first(0)
     from_two(8)
     from_core(7)
     terms(2, False)
-    x_first(0)
+    send_near(2)
+    x_first(1)
     aggregate(-1)
     partial(2)
-    x_first(1)
+    partial(3)
     aggregate(1)
-    partial(3)
-    partial(4)
     x_first(2)
-    partial(5)
-    x_first(3)
-    partial(6)
-    aggregate(2)
-    x_first(4)
-    partial(7)
-    x_first(5)
     in_moment.wait()
     in_second.wait()
     adam(0)
+    partial(4)
+    x_first(3)
     x_second(0)
+    partial(5)
+    x_first(4)
+    x_second(1)
+    aggregate(2)
+    partial(6)
+    x_first(5)
+    adam(-1)
+    adam(1)
+    partial(7)
     x_first(6)
-    x_second(1)
-    adam(-1)
+    x_second(2)
     x_first(7)
-    x_second(2)
-    adam(1)
     x_second(3)
+    relay(0)
     adam(2)
-    relay(0)
+    relay(-1)
+    relay(1)
     x_second(4)
-    relay(-1)
+    x_second(5)
+    relay(2)
     x_last(0)
-    x_second(5)
-    relay(1)
     x_last(1)
     x_second(6)
-    relay(2)
+    x_second(7)
     gathered(0)
     x_last(2)
     x_last(3)
-    x_second(7)
     gathered(-1)
+    gathered(1)
     x_last(4)
     x_last(5)
-    gathered(1)
+    gathered(2)
     x_last(6)
     x_last(7)
-    gathered(2)
     left(inc, GATHER)
     left(term.at[:, pl.ds(0, 15 * ROWS)], TERMS)
     left(fresh.at[:, pl.ds(0, 15 * ROWS)], NEW)
@@ -420,6 +450,7 @@
         out_specs=(pl.BlockSpec(memory_space=pltpu.VMEM),) * 4,
         scratch_shapes=[
             pltpu.VMEM((2 * X, TOK, 128), BF16),
+            pltpu.VMEM((TOK, 128), BF16),
             pltpu.VMEM((TOK, HW), BF16),
             pltpu.VMEM((HW, TOK), BF16),
             pltpu.VMEM((TOK, HW), F32),
@@ -433,8 +464,8 @@
             pltpu.VMEM((3, TOK, 128), BF16),
             pltpu.VMEM((2, TOK, 128), BF16),
             pltpu.VMEM((X, HW, COLS), BF16),
-            pltpu.VMEM((X, 3, 2 * ROWS, COLS), BF16),
-            pltpu.VMEM((X, 9, ROWS, COLS), BF16),
+            pltpu.VMEM((X, 8, ROWS, COLS), BF16),
+            pltpu.VMEM((X, 7, ROWS, COLS), BF16),
             pltpu.VMEM((X, HW, COLS), F32),
             pltpu.SemaphoreType.DMA((PIECES,)),
             pltpu.SemaphoreType.DMA((PIECES,)),
@@ -448,7 +479,7 @@
             pltpu.SemaphoreType.DMA((X,)),
             pltpu.SemaphoreType.DMA((X,)),
             pltpu.SemaphoreType.DMA((4,)),
-            pltpu.SemaphoreType.DMA((5,)),
+            pltpu.SemaphoreType.DMA((6,)),
         ],
         compiler_params=pltpu.CompilerParams(
             collective_id=0, has_side_effects=True, vmem_limit_bytes=56 * 1024 * 1024

time: 62.6 us -> 59.6 us (0.952)
  Pallas kernels: 61.9 us -> 58.8 us
    pallas_call x1, Pallas kernels: 60.6 us -> 57.5 us  [on_device(): pl.pallas_call(kernel, out_shape=(pltpu.VMEM((TOK, 128), BF16), pltpu.VME...]
where the time goes in v4:
time: 59.6 us; the launch traced here: 59.5 us
  Pallas kernels  58.8 us (99%)
  between operations  0.64 us (1%)
    pallas_call x1, Pallas kernels, on_device(): pl.pallas_call(kernel, out_shape=(pltpu.VMEM((TOK, 128), BF16), pltpu.VME...  57.5 us
    pallas_call x1, Pallas kernels, on_device(): pl.pallas_call(place, out_shape=shapes, in_specs=[pl.BlockSpec(memory_spa...  1.28 us

profile of v4, /device:TPU:1, one launch (start us, length us, event | category | flops | bytes accessed | tf_op | source)
XLA Modules:
  0.0 59.5 jit_solution(3042384206454425232)
XLA Ops:
  0.6 57.5 %shard_map.93 = (bf16[2048,128]{1,0:T(8,128)(2,1)S(1)}, bf16[4,512,256]{2,1,0:T(8,128)(2,1)S(1)}, f32[32,1024]{1,0:T(8,128)S(1)}, f32[32,1024]{1,0:T(8,128)S(1)}) custom-call(bf16[1,2048,128]{2,1,0:T(8,128)(2,1)} %handoff.1, bf16[1,2048,512]{2,1,0:T(8,128)(2,1)} %pre_in.1, bf16[1,512,1024]{2,1,0:T(8,128)(2,1)} %down_in.1, bf16[1,512,1024]{2,1,0:T(8,128)(2,1)} %up_in.1, ...), custom_call_target="tpu_custom_call" | custom-call | flops 6442450944 | bytes 12582912 | tf_op jit(solution)/shard_map/pallas_call | solution.py:441
  58.2 1.3 %shard_map.94 = (bf16[1,2048,128]{2,1,0:T(8,128)(2,1)}, bf16[1,512,1024]{2,1,0:T(8,128)(2,1)}, f32[1,32,1024]{2,1,0:T(8,128)}, f32[1,32,1024]{2,1,0:T(8,128)}) custom-call(bf16[2048,128]{1,0:T(8,128)(2,1)S(1)} %get-tuple-element.8.grad, bf16[4,512,256]{2,1,0:T(8,128)(2,1)S(1)} %get-tuple-element.9.fresh, f32[32,1024]{1,0:T(8,128)S(1)} %get-tuple-element.10.moment, ...), custom_call_target="tpu_custom_call" | custom-call | tf_op jit(solution)/shard_map/pallas_call | solution.py:489

commit v5 on v4

--- a/solution.py
+++ b/solution.py
@@ -34,7 +34,7 @@
     part, part_got, two_got, one_send, one_got,
     term, agg_got, fin_got, so_far,
     y_sem, x_sem, two_sem, core_sem, pair_sem, far_sem, last_sem,
-    agg_sem, fin_sem, ring_sem, row_sem, send_sem, local,
+    agg_sem, fin_sem, ring_sem, tail_sem, row_sem, send_sem, local,
 ):
     p = lax.axis_index("pipe")
     d = lax.axis_index("dp")
@@ -151,14 +151,13 @@
         share(2, s)
         share(2, s + 1)
 
-    for s in range(PIECES):
-        put(hand_here.at[piece(s)], inc.at[t, piece(s)], across, GATHER, y_sem.at[s])
-    in_down = move(down_in.at[0], down)
-    in_up = move(up_in.at[0], up)
-    in_moment = move(moment_in.at[0], moment)
-    in_second = move(second_in.at[0], second)
+    def send_y():
+        for s in range(PIECES):
+            put(hand_here.at[piece(s)], inc.at[t, piece(s)], across, GATHER, y_sem.at[s])
+
 
     GELU = 128
+    LEAD = 6
 
     def gelu(first, last):
         def body(b, carry):
@@ -243,23 +242,34 @@
             put(block, block, owner(step, h), NEW, row_sem.at[xa])
         put(block, block, owner(0, 1), NEW, row_sem.at[xa])
 
+    def pass_rows(xa, h, step, sides):
+        half = ROWS // 2
+        start = (at_z(-2 * step) * 2 + at_h(h)) * ROWS + (0 if step == 1 else half)
+        part_rows = fresh.at[xa, pl.ds(pl.multiple_of(start, half), half)]
+        block = fresh.at[xa, rows_of(-2 * step, h)]
+        for side in sides:
+            put(part_rows, part_rows, owner(2 * step, side), NEW, row_sem.at[xa])
+        for side in sides:
+            put(block, block, owner(step, side), NEW, row_sem.at[xa])
+
     def relay(k):
         xa = at_x(k)
         landed(fresh.at[xa, pl.ds(0, 2 * ROWS)], ring_sem.at[xa])
-        half = ROWS // 2
-        for step, first in ((1, 0), (-1, half)):
+        for step in (1, -1):
             block = fresh.at[xa, rows_of(-2 * step, 0)]
-            start = (at_z(-2 * step) * 2 + yh) * ROWS + first
-            part_rows = fresh.at[xa, pl.ds(pl.multiple_of(start, half), half)]
-            for h in (1, 0):
-                put(part_rows, part_rows, owner(2 * step, h), NEW, row_sem.at[xa])
-            for h in (1, 0):
-                put(block, block, owner(step, h), NEW, row_sem.at[xa])
-            put(block, block, owner(0, 1), NEW, row_sem.at[xa])
+            put(block, block, owner(0, 1), NEW, (row_sem if k == 2 else tail_sem).at[xa])
+        for step in (1, -1):
+            pass_rows(xa, 0, step, (1, 0) if k == 2 else (0,))
+
+    def cross(k):
+        xa = at_x(k)
+        landed(fresh.at[xa, pl.ds(0, 2 * ROWS)], tail_sem.at[xa])
+        for step in (1, -1):
+            pass_rows(xa, 1, step, (0,))
 
     def gathered(k):
         xa = at_x(k)
-        landed(fresh.at[xa, pl.ds(0, 13 * ROWS)], row_sem.at[xa])
+        landed(fresh.at[xa, pl.ds(0, (13 if k == 2 else 11) * ROWS)], row_sem.at[xa])
 
     def chunk(i):
         return pl.ds(i * CHUNK, CHUNK)
@@ -305,19 +315,25 @@
         both = one_got[0, rows].astype(F32) + one_got[1, rows].astype(F32)
         grad[rows] = (summed(i, 0) + both).astype(BF16)
 
+    ahead = LEAD * c
+    in_pre.wait()
+    gelu(0, ahead)
+    send_y()
+    in_down = move(down_in.at[0], down)
+    in_up = move(up_in.at[0], up)
+    in_moment = move(moment_in.at[0], moment)
+    in_second = move(second_in.at[0], second)
+    gelu(ahead, LEAD)
     from_y(0)
-    in_pre.wait()
-    gelu(0, 2)
     from_y(1)
-    gelu(2, 6)
+    gelu(LEAD, 9)
     from_y(2)
-    gelu(6, 10)
+    gelu(9, 12)
     from_y(3)
     from_x(0)
-    gelu(10, 14)
+    gelu(12, 16)
     from_y(4)
     from_x(1)
-    gelu(14, 16)
     from_y(5)
     from_x(2)
     from_y(6)
@@ -358,19 +374,20 @@
     from_two(4)
     partial(0)
     from_two(6)
-    aggregate(0)
     from_core(5)
-    partial(1)
+    pl.when(c == 1)(lambda: partial(1))
     from_core(6)
     terms(2, True)
+    aggregate(0)
     x_first(0)
     from_two(8)
     from_core(7)
     terms(2, False)
     send_near(2)
-    x_first(1)
+    pl.when(c == 0)(lambda: partial(1))
     aggregate(-1)
     partial(2)
+    x_first(1)
     partial(3)
     aggregate(1)
     x_first(2)
@@ -379,29 +396,32 @@
     adam(0)
     partial(4)
     x_first(3)
+    aggregate(2)
     x_second(0)
     partial(5)
     x_first(4)
-    x_second(1)
-    aggregate(2)
+    adam(-1)
     partial(6)
     x_first(5)
-    adam(-1)
     adam(1)
+    x_second(1)
     partial(7)
     x_first(6)
-    x_second(2)
-    x_first(7)
-    x_second(3)
     relay(0)
     adam(2)
+    x_first(7)
+    x_second(2)
+    x_second(3)
     relay(-1)
+    cross(0)
     relay(1)
     x_second(4)
+    relay(2)
     x_second(5)
-    relay(2)
+    cross(-1)
     x_last(0)
     x_last(1)
+    cross(1)
     x_second(6)
     x_second(7)
     gathered(0)
@@ -478,6 +498,7 @@
             pltpu.SemaphoreType.DMA((X,)),
             pltpu.SemaphoreType.DMA((X,)),
             pltpu.SemaphoreType.DMA((X,)),
+            pltpu.SemaphoreType.DMA((X,)),
             pltpu.SemaphoreType.DMA((4,)),
             pltpu.SemaphoreType.DMA((6,)),
         ],

time: 59.6 us -> 58 us (0.973)
  Pallas kernels: 58.8 us -> 57.2 us
    pallas_call x1, Pallas kernels: 57.5 us -> 55.9 us  [on_device(): pl.pallas_call(kernel, out_shape=(pltpu.VMEM((TOK, 128), BF16), pltpu.VME...]
where the time goes in v5:
time: 58 us; the launch traced here: 57.9 us
  Pallas kernels  57.2 us (99%)
  between operations  0.64 us (1%)
    pallas_call x1, Pallas kernels, on_device(): pl.pallas_call(kernel, out_shape=(pltpu.VMEM((TOK, 128), BF16), pltpu.VME...  55.9 us
    pallas_call x1, Pallas kernels, on_device(): pl.pallas_call(place, out_shape=shapes, in_specs=[pl.BlockSpec(memory_spa...  1.28 us

profile of v5, /device:TPU:1, one launch (start us, length us, event | category | flops | bytes accessed | tf_op | source)
XLA Modules:
  0.0 57.9 jit_solution(16009847902380993042)
XLA Ops:
  0.6 55.9 %shard_map.93 = (bf16[2048,128]{1,0:T(8,128)(2,1)S(1)}, bf16[4,512,256]{2,1,0:T(8,128)(2,1)S(1)}, f32[32,1024]{1,0:T(8,128)S(1)}, f32[32,1024]{1,0:T(8,128)S(1)}) custom-call(bf16[1,2048,128]{2,1,0:T(8,128)(2,1)} %handoff.1, bf16[1,2048,512]{2,1,0:T(8,128)(2,1)} %pre_in.1, bf16[1,512,1024]{2,1,0:T(8,128)(2,1)} %down_in.1, bf16[1,512,1024]{2,1,0:T(8,128)(2,1)} %up_in.1, ...), custom_call_target="tpu_custom_call" | custom-call | flops 6442450944 | bytes 12582912 | tf_op jit(solution)/shard_map/pallas_call | solution.py:461
  56.6 1.3 %shard_map.94 = (bf16[1,2048,128]{2,1,0:T(8,128)(2,1)}, bf16[1,512,1024]{2,1,0:T(8,128)(2,1)}, f32[1,32,1024]{2,1,0:T(8,128)}, f32[1,32,1024]{2,1,0:T(8,128)}) custom-call(bf16[2048,128]{1,0:T(8,128)(2,1)S(1)} %get-tuple-element.8.grad, bf16[4,512,256]{2,1,0:T(8,128)(2,1)S(1)} %get-tuple-element.9.fresh, f32[32,1024]{1,0:T(8,128)S(1)} %get-tuple-element.10.moment, ...), custom_call_target="tpu_custom_call" | custom-call | tf_op jit(solution)/shard_map/pallas_call | solution.py:510

commit v6 on v5

--- a/solution.py
+++ b/solution.py
@@ -30,7 +30,7 @@
 def kernel(
     handoff, pre_in, down_in, up_in, moment_in, second_in,
     grad, fresh, new_m, new_v,
-    inc, hand_here, pre, hidden_t, slope, down, up, moment, second,
+    inc, hand_here, pre, hidden_t, slope, down, down_t, up, moment, second,
     part, part_got, two_got, one_send, one_got,
     term, agg_got, fin_got, so_far,
     y_sem, x_sem, two_sem, core_sem, pair_sem, far_sem, last_sem,
@@ -157,7 +157,7 @@
 
 
     GELU = 128
-    LEAD = 6
+    LEAD = 4
 
     def gelu(first, last):
         def body(b, carry):
@@ -257,9 +257,9 @@
         landed(fresh.at[xa, pl.ds(0, 2 * ROWS)], ring_sem.at[xa])
         for step in (1, -1):
             block = fresh.at[xa, rows_of(-2 * step, 0)]
-            put(block, block, owner(0, 1), NEW, (row_sem if k == 2 else tail_sem).at[xa])
+            put(block, block, owner(0, 1), NEW, (row_sem if k > 0 else tail_sem).at[xa])
         for step in (1, -1):
-            pass_rows(xa, 0, step, (1, 0) if k == 2 else (0,))
+            pass_rows(xa, 0, step, (1, 0) if k > 0 else (0,))
 
     def cross(k):
         xa = at_x(k)
@@ -269,15 +269,19 @@
 
     def gathered(k):
         xa = at_x(k)
-        landed(fresh.at[xa, pl.ds(0, (13 if k == 2 else 11) * ROWS)], row_sem.at[xa])
+        landed(fresh.at[xa, pl.ds(0, (13 if k > 0 else 11) * ROWS)], row_sem.at[xa])
 
     def chunk(i):
         return pl.ds(i * CHUNK, CHUNK)
+
+    def turn(n):
+        rows = pl.ds(n * 128, 128)
+        down_t[:, rows] = down[rows, :].T
 
     def partial(i):
         rows = chunk(i)
         block = jnp.concatenate([inc[s, rows] for s in range(2 * X)], axis=1)
-        back = lax.dot_general(block, down[...], (((1,), (1,)), ((), ())), preferred_element_type=F32)
+        back = jnp.dot(block, down_t[...], preferred_element_type=F32)
         act = (back * (1.0 / math.sqrt(D)) * slope[rows, :]).astype(BF16)
         value = jnp.dot(act, up[...], preferred_element_type=F32) * (1.0 / math.sqrt(FF))
         value = value.astype(BF16)
@@ -334,17 +338,26 @@
     gelu(12, 16)
     from_y(4)
     from_x(1)
+    in_down.wait()
+    turn(0)
     from_y(5)
     from_x(2)
+    turn(1)
     from_y(6)
     from_x(3)
+    turn(2)
     from_y(7)
     from_x(4)
+    turn(3)
     from_y(8)
     from_x(5)
     from_y(9)
-    for s in range(6):
-        pass_on(s)
+    pass_on(0)
+    pass_on(1)
+    pass_on(2)
+    pass_on(3)
+    pass_on(4)
+    pass_on(5)
     from_core(0)
     terms(0, True)
     from_x(6)
@@ -368,7 +381,6 @@
     terms(1, False)
     send_near(-1)
     send_near(1)
-    in_down.wait()
     in_up.wait()
     from_core(4)
     from_two(4)
@@ -396,40 +408,39 @@
     adam(0)
     partial(4)
     x_first(3)
-    aggregate(2)
-    x_second(0)
     partial(5)
     x_first(4)
     adam(-1)
+    aggregate(2)
+    x_second(0)
     partial(6)
     x_first(5)
+    x_second(1)
     adam(1)
-    x_second(1)
     partial(7)
     x_first(6)
     relay(0)
+    x_first(7)
     adam(2)
-    x_first(7)
     x_second(2)
     x_second(3)
     relay(-1)
-    cross(0)
     relay(1)
     x_second(4)
+    cross(0)
     relay(2)
     x_second(5)
     cross(-1)
     x_last(0)
     x_last(1)
-    cross(1)
     x_second(6)
     x_second(7)
     gathered(0)
     x_last(2)
     x_last(3)
     gathered(-1)
+    x_last(4)
     gathered(1)
-    x_last(4)
     x_last(5)
     gathered(2)
     x_last(6)
@@ -475,6 +486,7 @@
             pltpu.VMEM((HW, TOK), BF16),
             pltpu.VMEM((TOK, HW), F32),
             pltpu.VMEM((HW, D), BF16),
+            pltpu.VMEM((D, HW), BF16),
             pltpu.VMEM((HW, D), BF16),
             pltpu.VMEM((ROWS, D), F32),
             pltpu.VMEM((ROWS, D), F32),

time: 58 us -> 57.8 us (level)
  no operation moved by 1% of the time
where the time goes in v6:
time: 57.8 us; the launch traced here: 57.7 us
  Pallas kernels  57.1 us (99%)
  between operations  0.64 us (1%)
    pallas_call x1, Pallas kernels, on_device(): pl.pallas_call(kernel, out_shape=(pltpu.VMEM((TOK, 128), BF16), pltpu.VME...  55.8 us
    pallas_call x1, Pallas kernels, on_device(): pl.pallas_call(place, out_shape=shapes, in_specs=[pl.BlockSpec(memory_spa...  1.28 us

profile of v6, /device:TPU:1, one launch (start us, length us, event | category | flops | bytes accessed | tf_op | source)
XLA Modules:
  0.0 57.7 jit_solution(12808706652717743027)
XLA Ops:
  0.6 55.8 %shard_map.93 = (bf16[2048,128]{1,0:T(8,128)(2,1)S(1)}, bf16[4,512,256]{2,1,0:T(8,128)(2,1)S(1)}, f32[32,1024]{1,0:T(8,128)S(1)}, f32[32,1024]{1,0:T(8,128)S(1)}) custom-call(bf16[1,2048,128]{2,1,0:T(8,128)(2,1)} %handoff.1, bf16[1,2048,512]{2,1,0:T(8,128)(2,1)} %pre_in.1, bf16[1,512,1024]{2,1,0:T(8,128)(2,1)} %down_in.1, bf16[1,512,1024]{2,1,0:T(8,128)(2,1)} %up_in.1, ...), custom_call_target="tpu_custom_call" | custom-call | flops 6442450944 | bytes 12582912 | tf_op jit(solution)/shard_map/pallas_call | solution.py:472
  56.4 1.3 %shard_map.94 = (bf16[1,2048,128]{2,1,0:T(8,128)(2,1)}, bf16[1,512,1024]{2,1,0:T(8,128)(2,1)}, f32[1,32,1024]{2,1,0:T(8,128)}, f32[1,32,1024]{2,1,0:T(8,128)}) custom-call(bf16[2048,128]{1,0:T(8,128)(2,1)S(1)} %get-tuple-element.8.grad, bf16[4,512,256]{2,1,0:T(8,128)(2,1)S(1)} %get-tuple-element.9.fresh, f32[32,1024]{1,0:T(8,128)S(1)} %get-tuple-element.10.moment, ...), custom_call_target="tpu_custom_call" | custom-call | tf_op jit(solution)/shard_map/pallas_call | solution.py:522
